TPU v7x, 128 devices: a whole 4x4x4 slice. The times are simulated.
128 devices in a mesh: gx: 16 (over x, z_lo, core), gy: 8 (over y, z_hi).
Axes of the slice: x: 4, y: 4, z: 4 (z_hi: 2, z_lo: 2; z = z_hi * 2 + z_lo), core: 2. Of those that a mesh axis runs over, the one named last changes fastest.
Arguments:
- sources: float32 [262144, 128], P(('gx', 'gy')), may hold values from -6 to 6
- owner: int32 [262144, 1], P(('gx', 'gy')), may hold values from 0 to 127; in each aligned block of 2048 rows (0 to 2047, 2048 to 4095, ...) at most 32 rows name the same one
- box: int32 [262144], P(('gx', 'gy')), may hold values from 0 to 1023
- leaf_op: float32 [2, 64, 64], replicated, may hold values from -0.5 to 0.5
- level_ops: float32 [7, 2, 2, 2, 64, 64], replicated, may hold values from -0.375 to 0.375
- twiddle: float32 [7, 131072], P(None, ('gx', 'gy')), may hold values from -3.140625 to 3.140625
Outputs:
- weights: float32 [131072, 128], P(('gx', 'gy'))
Inputs may be any that keep to these rules, and one draw needn't show every extreme that they name: Among the 2048 source blocks of one device, at most 32 name the same owner; in every draw some device has exactly 32 for one owner.
All inputs are finite; a program needn't handle non-finite values.
Results may differ from a plain program's by a relative error of at most 0.0003.
Values sent between devices are 32-bit elements; how exact they have to be, the bound alone decides.
No kernel may reach another device: no remote copies, remote signals or barrier semaphores. Data moves between devices by JAX's collectives and lax.ppermute only.
A program may use at most 64 MiB of HBM per device.

v0:
```python
import jax
import jax.numpy as jnp
from jax import lax
from jax.sharding import PartitionSpec as P


def swapped(shard, axis, stride):
    return lax.ppermute(shard, axis, [(i, i ^ 1 << stride) for i in range(lax.axis_size(axis))])


def complex_block(parts):
    real = parts[0]
    imag = parts[1]
    upper = jnp.concatenate([real, imag], axis=1)
    lower = jnp.concatenate([-imag, real], axis=1)
    return jnp.concatenate([upper, lower], axis=0)


def level_matrix(ops):
    from_low = jnp.concatenate([complex_block(ops[0, 0]), complex_block(ops[1, 0])], axis=1)
    from_high = jnp.concatenate([complex_block(ops[0, 1]), complex_block(ops[1, 1])], axis=1)
    return jnp.concatenate([from_low, from_high], axis=0)


def rotate(blocks, angle):
    half = blocks.shape[-1] // 2
    real = blocks[:, :half]
    imag = blocks[:, half:]
    cosine = jnp.cos(angle)[:, None]
    sine = jnp.sin(angle)[:, None]
    return jnp.concatenate([real * cosine - imag * sine, real * sine + imag * cosine], axis=1)


def local(sources, owner, box, leaf_op, level_ops, twiddle):
    count_gx = lax.axis_size("gx")
    count_gy = lax.axis_size("gy")
    devices = count_gx * count_gy
    src_count = sources.shape[0]
    width = sources.shape[1]
    box_count = twiddle.shape[1]
    capacity = max(2, 2 * src_count // devices)
    destination = owner[:, 0]
    onehot = (destination[:, None] == jnp.arange(devices, dtype=jnp.int32)[None, :]).astype(
        jnp.int32
    )
    ranking = jnp.sum(jnp.cumsum(onehot, axis=0) * onehot, axis=1) - 1
    slot_index = destination * capacity + ranking
    packed = jnp.zeros((devices * capacity, width), jnp.float32).at[slot_index].set(sources)
    labels = jnp.full((devices * capacity,), box_count, jnp.int32).at[slot_index].set(box)
    arrived, arrived_labels = (
        lax.all_to_all(
            packed.reshape(devices, capacity, width),
            ("gx", "gy"),
            split_axis=0,
            concat_axis=0,
            tiled=True,
        ),
        lax.all_to_all(
            labels.reshape(devices, capacity), ("gx", "gy"), split_axis=0, concat_axis=0, tiled=True
        ),
    )
    gathered = jax.ops.segment_sum(
        arrived.reshape(-1, width), arrived_labels.reshape(-1), num_segments=box_count + 1
    )[:box_count]
    blocks = jnp.dot(
        gathered,
        complex_block(leaf_op),
        precision=lax.Precision.HIGHEST,
        preferred_element_type=jnp.float32,
    )
    bits_gy = count_gy.bit_length() - 1
    bits_gx = count_gx.bit_length() - 1
    for level in range(bits_gy + bits_gx):
        halves = blocks.reshape(2, box_count // 2, width)
        if level < bits_gy:
            parity = jnp.bitwise_and(jnp.right_shift(lax.axis_index("gy"), level), 1)
        else:
            parity = jnp.bitwise_and(jnp.right_shift(lax.axis_index("gx"), level - bits_gy), 1)
        upper_kept = parity == 1
        kept = jnp.where(upper_kept, halves[1], halves[0])
        outgoing = jnp.where(upper_kept, halves[0], halves[1])
        if level < bits_gy:
            incoming = swapped(outgoing, "gy", level)
        else:
            incoming = swapped(outgoing, "gx", level - bits_gy)
        lower = jnp.where(upper_kept, incoming, kept)
        upper = jnp.where(upper_kept, kept, incoming)
        stacked = jnp.concatenate([lower, upper], axis=1)
        mixed = jnp.dot(
            stacked,
            level_matrix(level_ops[level]),
            precision=lax.Precision.HIGHEST,
            preferred_element_type=jnp.float32,
        )
        blocks = rotate(mixed.reshape(box_count, width), twiddle[level])
    return blocks


def solution(mesh):
    in_specs = (
        P(("gx", "gy"), None),
        P(("gx", "gy"), None),
        P(("gx", "gy")),
        P(),
        P(),
        P(None, ("gx", "gy")),
    )
    out_specs = P(("gx", "gy"), None)
    return jax.shard_map(local, mesh=mesh, in_specs=in_specs, out_specs=out_specs, check_vma=False)
```

profile of v0, /device:TPU:1, one launch (start us, length us, event | category | flops | bytes accessed | tf_op | source)
XLA Modules:
  0.0 157.8 jit_solution(11188473466795456148)
XLA Ops:
  0.0 0.8 copy.10
  0.8 0.3 fusion.3
  1.2 0.1 broadcast_add_fusion
  1.3 0.3 copy.11
  1.6 0.3 copy-done.6
  1.9 0.6 fusion
  2.6 8.2 %scatter_custom_fusion = s32[4096]{0:T(1024)S(1)} fusion(s32[2048]{0:T(1024)S(1)} %bitcast.235, s32[2048]{0:T(1024)} %param.8, s32[]{:T(128)} %constant.30.clone.1), kind=kCustom, calls=%fused_computation.403 | custom fusion | bytes 16896 | tf_op jit(solution)/shard_map/scatter | solution.py:49
  10.8 0.7 all_to_all.9
  11.5 11.5 %all-to-all-start = ((s32[128,1,32]{2,1,0:T(1,128)}), s32[128,1,32]{2,1,0:T(1,128)S(1)}, u32[]{:S(2)}, u32[]{:S(2)}) async-start(s32[128,1,32]{2,1,0:T(1,128)} %bitcast.7), calls=%async_computation | async-start | bytes 131072 | tf_op jit(solution)/shard_map/all_to_all | solution.py:58
  23.0 7.4 %scatter_custom_fusion.1 = f32[4096,128]{1,0:T(8,128)} fusion(s32[2048]{0:T(1024)S(1)} %bitcast.236, f32[2048,128]{1,0:T(8,128)} %param.6, f32[]{:T(128)} %constant.11.clone.1), kind=kCustom, calls=%fused_computation.5 | custom fusion | bytes 2097664 | tf_op jit(solution)/shard_map/scatter | solution.py:48
  30.4 2.4 %all-to-all-done = s32[128,1,32]{2,1,0:T(1,128)S(1)} async-done(((s32[128,1,32]{2,1,0:T(1,128)}), s32[128,1,32]{2,1,0:T(1,128)S(1)}, u32[]{:S(2)}, u32[]{:S(2)}) %all-to-all-start) | async-done | bytes 16416 | tf_op jit(solution)/shard_map/all_to_all | solution.py:58
  32.8 7.4 %all-to-all-start.1 = ((f32[128,32,128]{2,1,0:T(8,128)}), f32[128,32,128]{2,1,0:T(8,128)S(1)}, u32[]{:S(2)}, u32[]{:S(2)}) async-start(f32[128,32,128]{2,1,0:T(8,128)} %bitcast.8), calls=%async_computation.1 | async-start | bytes 4194304 | tf_op jit(solution)/shard_map/all_to_all | solution.py:51
  40.2 2.4 %slice_bitcast_fusion = (f32[2,2,2,64,64]{4,3,2,1,0:T(8,128)S(1)}, f32[2,2,2,64,64]{4,3,2,1,0:T(8,128)S(1)}, f32[2,2,2,64,64]{4,3,2,1,0:T(8,128)}, f32[2,2,2,64,...) fusion(f32[7,2,2,2,64,64]{5,4,3,2,1,0:T(8,128)} %param.10), kind=kLoop, calls=%fused_computation.301 | loop fusion | bytes 1835008 | tf_op jit(solution)/shard_map/squeeze | solution.py:91
  42.6 0.7 fusion.279
  43.3 0.5 broadcast.48
  43.8 0.7 reduce.3
  44.6 0.7 reshape.316
  45.2 25.4 %all-to-all-done.1 = f32[128,32,128]{2,1,0:T(8,128)S(1)} async-done(((f32[128,32,128]{2,1,0:T(8,128)}), f32[128,32,128]{2,1,0:T(8,128)S(1)}, u32[]{:S(2)}, u32[]{:S(2)}) %all-to-all-start.1) | async-done | bytes 2097184 | tf_op jit(solution)/shard_map/all_to_all | solution.py:51
  70.6 22.8 %scatter_custom_fusion.2 = f32[1025,128]{1,0:T(8,128)S(1)} fusion(s32[4096]{0:T(1024)} %reshape.316, f32[4096,128]{1,0:T(8,128)S(1)} %bitcast.217, f32[]{:T(128)} %constant.11.clone.1), kind=kCustom, calls=%fused_computation.70 | custom fusion | flops 524288 | bytes 525312 | tf_op jit(solution)/shard_map/scatter-add | solution.py:62
  93.5 0.7 fusion.5
  94.3 1.4 collective-permute-start
  95.7 1.8 %slice_cosine_fusion = (f32[1,1024]{1,0:T(1,128)S(1)}, f32[1,1024]{1,0:T(1,128)S(1)}, f32[1,1024]{1,0:T(1,128)S(1)}, f32[1,1024]{1,0:T(1,128)S(1)}, f32[1,1024]{...) fusion(f32[7,1024]{1,0:T(8,128)} %param.11), kind=kLoop, calls=%fused_computation.407 | loop fusion | bytes 86016 | tf_op jit(solution)/shard_map/cos | solution.py:29
  97.5 6.6 %collective-permute-done = f32[512,128]{0,1:T(8,128)S(1)} collective-permute-done((f32[512,128]{0,1:T(8,128)S(1)}, f32[512,128]{0,1:T(8,128)S(1)}, u32[]{:S(2)}, u32[]{:S(2)}) %collective-permute-start) | collective-permute-done | bytes 262176 | tf_op jit(solution)/shard_map/ppermute | solution.py:8
  104.2 0.1 broadcast_select_fusion.1
  104.3 1.1 fusion.7
  105.4 0.5 multiply_subtract_fusion.6
  105.9 0.2 broadcast_select_fusion.5
  106.1 0.3 collective-permute-start.1
  106.5 7.4 %collective-permute-done.1 = f32[512,128]{1,0:T(8,128)S(1)} collective-permute-done((f32[512,128]{1,0:T(8,128)S(1)}, f32[512,128]{1,0:T(8,128)S(1)}, u32[]{:S(2)}, u32[]{:S(2)}) %collective-permute-start.1) | collective-permute-done | bytes 262176 | tf_op jit(solution)/shard_map/ppermute | solution.py:8
  113.9 0.2 broadcast_select_fusion.3
  114.1 0.7 fusion.11
  114.9 0.5 multiply_subtract_fusion.5
  115.4 0.2 broadcast_select_fusion.9
  115.6 0.1 collective-permute-start.2
  115.7 0.2 copy-done.1
  115.9 7.8 %collective-permute-done.2 = f32[512,128]{1,0:T(8,128)S(1)} collective-permute-done((f32[512,128]{1,0:T(8,128)S(1)}, f32[512,128]{1,0:T(8,128)S(1)}, u32[]{:S(2)}, u32[]{:S(2)}) %collective-permute-start.2) | collective-permute-done | bytes 262176 | tf_op jit(solution)/shard_map/ppermute | solution.py:8
  123.7 0.2 broadcast_select_fusion.7
  123.9 0.7 fusion.15
  124.7 0.5 multiply_subtract_fusion.4
  125.2 0.2 broadcast_select_fusion.13
  125.4 2.2 %collective-permute-start.3 = (f32[512,128]{1,0:T(8,128)S(1)}, f32[512,128]{1,0:T(8,128)S(1)}, u32[]{:S(2)}, u32[]{:S(2)}) collective-permute-start(f32[512,128]{1,0:T(8,128)S(1)} %get-tuple-element.11), channel_id=1, source_target_pairs={{0,8},{8,0},{16,24},{24,16},{32,40},{40,32},{48,56},{56,48},{64,72... | collective-permute-start | bytes 786440 | tf_op jit(solution)/shard_map/ppermute | solution.py:8
  127.7 1.1 collective-permute-done.3
  128.8 0.2 broadcast_select_fusion.11
  129.0 0.7 fusion.19
  129.8 0.5 multiply_subtract_fusion.3
  130.3 0.2 broadcast_select_fusion.17
  130.5 1.0 collective-permute-start.4
  131.5 6.5 %collective-permute-done.4 = f32[512,128]{1,0:T(8,128)S(1)} collective-permute-done((f32[512,128]{1,0:T(8,128)S(1)}, f32[512,128]{1,0:T(8,128)S(1)}, u32[]{:S(2)}, u32[]{:S(2)}) %collective-permute-start.4) | collective-permute-done | bytes 262176 | tf_op jit(solution)/shard_map/ppermute | solution.py:8
  138.1 0.2 broadcast_select_fusion.15
  138.3 0.7 fusion.23
  139.1 0.5 multiply_subtract_fusion.2
  139.5 0.2 broadcast_select_fusion.21
  139.8 0.9 collective-permute-start.5
  140.7 5.7 %collective-permute-done.5 = f32[512,128]{1,0:T(8,128)S(1)} collective-permute-done((f32[512,128]{1,0:T(8,128)S(1)}, f32[512,128]{1,0:T(8,128)S(1)}, u32[]{:S(2)}, u32[]{:S(2)}) %collective-permute-start.5) | collective-permute-done | bytes 262176 | tf_op jit(solution)/shard_map/ppermute | solution.py:8
  146.4 0.2 broadcast_select_fusion.19
  146.6 0.7 fusion.27
  147.4 0.5 multiply_subtract_fusion.1
  147.9 0.2 broadcast_select_fusion.25
  148.1 1.9 %collective-permute-start.6 = (f32[512,128]{1,0:T(8,128)S(1)}, f32[512,128]{1,0:T(8,128)S(1)}, u32[]{:S(2)}, u32[]{:S(2)}) collective-permute-start(f32[512,128]{1,0:T(8,128)S(1)} %get-tuple-element.5), channel_id=1, source_target_pairs={{0,64},{8,72},{16,80},{24,88},{32,96},{40,104},{48,112},{56,120},{... | collective-permute-start | bytes 786440 | tf_op jit(solution)/shard_map/ppermute | solution.py:8
  150.0 5.4 %collective-permute-done.6 = f32[512,128]{1,0:T(8,128)S(1)} collective-permute-done((f32[512,128]{1,0:T(8,128)S(1)}, f32[512,128]{1,0:T(8,128)S(1)}, u32[]{:S(2)}, u32[]{:S(2)}) %collective-permute-start.6) | collective-permute-done | bytes 262176 | tf_op jit(solution)/shard_map/ppermute | solution.py:8
  155.4 0.2 broadcast_select_fusion.23
  155.6 0.7 fusion.31
  156.3 0.5 multiply_subtract_fusion
  156.8 1.0 pad_maximum_fusion
  (46 shorter events, 0.6 us)
Async XLA Ops:
  1.2 0.7 copy-start.6
  11.5 21.3 %all-to-all-start = ((s32[128,1,32]{2,1,0:T(1,128)}), s32[128,1,32]{2,1,0:T(1,128)S(1)}, u32[]{:S(2)}, u32[]{:S(2)}) async-start(s32[128,1,32]{2,1,0:T(1,128)} %bitcast.7), calls=%async_computation | async-start | bytes 131072 | tf_op jit(solution)/shard_map/all_to_all | solution.py:58
  32.8 7.4 %copy-start.5 = (f32[2,64,64]{2,1,0:T(8,128)S(1)}, f32[2,64,64]{2,1,0:T(8,128)}, u32[]{:S(2)}) copy-start(f32[2,64,64]{2,1,0:T(8,128)} %param.9) | copy-start | bytes 98308
  32.8 37.8 %all-to-all-start.1 = ((f32[128,32,128]{2,1,0:T(8,128)}), f32[128,32,128]{2,1,0:T(8,128)S(1)}, u32[]{:S(2)}, u32[]{:S(2)}) async-start(f32[128,32,128]{2,1,0:T(8,128)} %bitcast.8), calls=%async_computation.1 | async-start | bytes 4194304 | tf_op jit(solution)/shard_map/all_to_all | solution.py:51
  42.6 28.0 %copy-start.3 = (f32[2,2,2,64,64]{4,3,2,1,0:T(8,128)}, f32[2,2,2,64,64]{4,3,2,1,0:T(8,128)S(1)}, u32[]{:S(2)}) copy-start(f32[2,2,2,64,64]{4,3,2,1,0:T(8,128)S(1)} %get-tuple-element.22) | copy-start | bytes 393220
  93.5 4.0 %copy-start.4 = (f32[2,2,2,64,64]{4,3,2,1,0:T(8,128)S(1)}, f32[2,2,2,64,64]{4,3,2,1,0:T(8,128)}, u32[]{:S(2)}) copy-start(f32[2,2,2,64,64]{4,3,2,1,0:T(8,128)} %copy-done.3) | copy-start | bytes 393220
  93.5 10.7 %copy-start.7 = (f32[64,64]{1,0:T(8,128)S(1)}, f32[64,64]{1,0:T(8,128)}, u32[]{:S(2)}) copy-start(f32[64,64]{1,0:T(8,128)} %get-tuple-element.133) | copy-start | bytes 49156
  93.5 10.7 %copy-start.8 = (f32[64,64]{1,0:T(8,128)S(1)}, f32[64,64]{1,0:T(8,128)}, u32[]{:S(2)}) copy-start(f32[64,64]{1,0:T(8,128)} %get-tuple-element.134) | copy-start | bytes 49156
  93.5 10.7 %copy-start.9 = (f32[64,64]{1,0:T(8,128)S(1)}, f32[64,64]{1,0:T(8,128)}, u32[]{:S(2)}) copy-start(f32[64,64]{1,0:T(8,128)} %get-tuple-element.135) | copy-start | bytes 49156
  94.3 9.9 %collective-permute-start = (f32[512,128]{0,1:T(8,128)S(1)}, f32[512,128]{0,1:T(8,128)S(1)}, u32[]{:S(2)}, u32[]{:S(2)}) collective-permute-start(f32[512,128]{0,1:T(8,128)S(1)} %slice_select_fusion.1), channel_id=1, source_target_pairs={{0,1},{1,0},{2,3},{3,2},{4,5},{5,4},{6,7},{7,6},{8,9},{9,8},{10,11... | collective-permute-start | bytes 786440 | tf_op jit(solution)/shard_map/ppermute | solution.py:8
  105.4 1.0 copy-start.2
  106.1 7.8 %collective-permute-start.1 = (f32[512,128]{1,0:T(8,128)S(1)}, f32[512,128]{1,0:T(8,128)S(1)}, u32[]{:S(2)}, u32[]{:S(2)}) collective-permute-start(f32[512,128]{1,0:T(8,128)S(1)} %get-tuple-element.15), channel_id=1, source_target_pairs={{0,2},{1,3},{2,0},{3,1},{4,6},{5,7},{6,4},{7,5},{8,10},{9,11},{10,... | collective-permute-start | bytes 786440 | tf_op jit(solution)/shard_map/ppermute | solution.py:8
  114.9 1.0 copy-start.1
  115.6 8.1 %collective-permute-start.2 = (f32[512,128]{1,0:T(8,128)S(1)}, f32[512,128]{1,0:T(8,128)S(1)}, u32[]{:S(2)}, u32[]{:S(2)}) collective-permute-start(f32[512,128]{1,0:T(8,128)S(1)} %get-tuple-element.13), channel_id=1, source_target_pairs={{0,4},{1,5},{2,6},{3,7},{4,0},{5,1},{6,2},{7,3},{8,12},{9,13},{10,... | collective-permute-start | bytes 786440 | tf_op jit(solution)/shard_map/ppermute | solution.py:8
  124.7 2.9 %copy-start = (f32[2,2,2,64,64]{4,3,2,1,0:T(8,128)S(1)}, f32[2,2,2,64,64]{4,3,2,1,0:T(8,128)}, u32[]{:S(2)}) copy-start(f32[2,2,2,64,64]{4,3,2,1,0:T(8,128)} %get-tuple-element.19) | copy-start | bytes 393220
  125.4 3.4 %collective-permute-start.3 = (f32[512,128]{1,0:T(8,128)S(1)}, f32[512,128]{1,0:T(8,128)S(1)}, u32[]{:S(2)}, u32[]{:S(2)}) collective-permute-start(f32[512,128]{1,0:T(8,128)S(1)} %get-tuple-element.11), channel_id=1, source_target_pairs={{0,8},{8,0},{16,24},{24,16},{32,40},{40,32},{48,56},{56,48},{64,72... | collective-permute-start | bytes 786440 | tf_op jit(solution)/shard_map/ppermute | solution.py:8
  130.5 7.6 %collective-permute-start.4 = (f32[512,128]{1,0:T(8,128)S(1)}, f32[512,128]{1,0:T(8,128)S(1)}, u32[]{:S(2)}, u32[]{:S(2)}) collective-permute-start(f32[512,128]{1,0:T(8,128)S(1)} %get-tuple-element.9), channel_id=1, source_target_pairs={{0,16},{8,24},{16,0},{24,8},{32,48},{40,56},{48,32},{56,40},{64,80... | collective-permute-start | bytes 786440 | tf_op jit(solution)/shard_map/ppermute | solution.py:8
  139.8 6.7 %collective-permute-start.5 = (f32[512,128]{1,0:T(8,128)S(1)}, f32[512,128]{1,0:T(8,128)S(1)}, u32[]{:S(2)}, u32[]{:S(2)}) collective-permute-start(f32[512,128]{1,0:T(8,128)S(1)} %get-tuple-element.7), channel_id=1, source_target_pairs={{0,32},{8,40},{16,48},{24,56},{32,0},{40,8},{48,16},{56,24},{64,96... | collective-permute-start | bytes 786440 | tf_op jit(solution)/shard_map/ppermute | solution.py:8
  148.1 7.3 %collective-permute-start.6 = (f32[512,128]{1,0:T(8,128)S(1)}, f32[512,128]{1,0:T(8,128)S(1)}, u32[]{:S(2)}, u32[]{:S(2)}) collective-permute-start(f32[512,128]{1,0:T(8,128)S(1)} %get-tuple-element.5), channel_id=1, source_target_pairs={{0,64},{8,72},{16,80},{24,88},{32,96},{40,104},{48,112},{56,120},{... | collective-permute-start | bytes 786440 | tf_op jit(solution)/shard_map/ppermute | solution.py:8
where the time goes:
time: 160 us; the launch traced here: 158 us
  waiting for transfers between devices  68.4 us (43%)
  other arithmetic  32.3 us (20%)
  starting transfers between devices  26.6 us (17%)
  local copies, waits for them, and re-layouts  23.8 us (15%)
  matrix products  6.15 us (4%)
    ppermute x7, waiting for transfers between devices, swapped(): lax.ppermute(shard, axis, [(i, i ^ 1 << stride) for i in range(lax.axis_s...  40.6 us
    all_to_all x1, waiting for transfers between devices, local(): lax.all_to_all(packed.reshape(devices, capacity, width), ('gx', 'gy'), sp...  25.4 us
    scatter-add x1, other arithmetic, local(): jax.ops.segment_sum(arrived.reshape(-1, width), arrived_labels.reshape(-1...  22.8 us
    all_to_all x1, starting transfers between devices, local(): lax.all_to_all(labels.reshape(devices, capacity), ('gx', 'gy'), split_axi...  11.5 us
    scatter x1, local copies, waits for them, and re-layouts, local(): jnp.full((devices * capacity,), box_count, jnp.int32).at[slot_index]  8.23 us
    ppermute x7, starting transfers between devices, swapped(): lax.ppermute(shard, axis, [(i, i ^ 1 << stride) for i in range(lax.axis_s...  7.74 us
    scatter x1, local copies, waits for them, and re-layouts, local(): jnp.zeros((devices * capacity, width), jnp.float32).at[slot_index]  7.41 us
    all_to_all x1, starting transfers between devices, local(): lax.all_to_all(packed.reshape(devices, capacity, width), ('gx', 'gy'), sp...  7.36 us
  transfers between devices with their start and end apart: 9, of which 9 were waited for; matrix products, arithmetic and copies ran while one was open for 9% of the time, Pallas kernels for 0%

commit v1 on v0

--- a/solution.py
+++ b/solution.py
@@ -1,7 +1,12 @@
 import jax
 import jax.numpy as jnp
 from jax import lax
+from jax.experimental import pallas as pl
+from jax.experimental.pallas import tpu as pltpu
 from jax.sharding import PartitionSpec as P
+
+LANES = 128
+VMEM_LIMIT = 48 * 1024 * 1024
 
 
 def swapped(shard, axis, stride):
@@ -31,7 +36,7 @@
     return jnp.concatenate([real * cosine - imag * sine, real * sine + imag * cosine], axis=1)
 
 
-def local(sources, owner, box, leaf_op, level_ops, twiddle):
+def general(sources, owner, box, leaf_op, level_ops, twiddle):
     count_gx = lax.axis_size("gx")
     count_gy = lax.axis_size("gy")
     devices = count_gx * count_gy
@@ -96,6 +101,403 @@
     return blocks
 
 
+SLOTS = 40
+KEPT = SLOTS - 1
+FLAG_LANE = 39
+FIRST_LANE = 48
+SECOND_LANE = 64
+UNROLL = 32
+
+
+def bit(value, place):
+    return jnp.bitwise_and(jnp.right_shift(value, place), 1)
+
+
+def bits_to(value, places):
+    total = None
+    for source, target in places:
+        term = jnp.left_shift(bit(value, source), target)
+        total = term if total is None else total + term
+    return total
+
+
+def iota(shape, axis):
+    return lax.broadcasted_iota(jnp.int32, shape, axis)
+
+
+def exact_dot(left, right, contract=(1, 0)):
+    return lax.dot_general(
+        left,
+        right,
+        (((contract[0],), (contract[1],)), ((), ())),
+        precision=lax.Precision.HIGHEST,
+        preferred_element_type=jnp.float32,
+    )
+
+
+def angles_for_all(twiddle_ref, level, lane):
+    width = 16 << level
+    devices = LANES
+    dest = iota((devices, LANES), 0)
+    cols = iota((devices, LANES), 1)
+    first = bits_to(dest, [(level + 1 + b, 2 - b) for b in range(3)])
+    last = range(level + 4, 7)
+    group = bits_to(dest, [(b, 6 - b) for b in last])
+    rows = jnp.zeros((devices, LANES), jnp.float32)
+    for g in range(8):
+        part = twiddle_ref[level : level + 1, g * LANES : (g + 1) * LANES]
+        rows = jnp.where(first == g, part, rows)
+    rows = jnp.where(jnp.right_shift(cols, 4 + level) == group, rows, 0.0)
+    fold = jnp.where(cols == lane + jnp.bitwise_and(dest, width - 1), 1.0, 0.0)
+    return exact_dot(rows, fold)
+
+
+def pack_kernel(owner_ref, box_ref, src_ref, twiddle_ref, out_ref, slot_vmem, slot_smem, sem):
+    chunks = owner_ref.shape[0]
+    devices = LANES
+    rows = iota((devices, LANES), 0)
+    cols = iota((devices, LANES), 1)
+    upto = jnp.where(rows <= cols, 1.0, 0.0).astype(jnp.bfloat16)
+    high_half = rows < 64
+    rank_of_row = jnp.bitwise_and(rows, 63)
+    places = [(0, 9), (1, 8), (2, 7), (4, 6), (5, 5), (3, 4), (6, 3)]
+
+    def rank_chunk(c, carried):
+        count, labels = carried
+        owner = owner_ref[pl.ds(c, 1), :]
+        box = box_ref[pl.ds(c, 1), :]
+        dest = bits_to(box, [(3 + b, 6 - b) for b in range(7)])
+        target = bits_to(owner, places) + jnp.bitwise_and(box, 7) + 1
+        hit = dest == rows
+        onehot = jnp.where(hit, 1.0, 0.0).astype(jnp.bfloat16)
+        upto_here = jnp.dot(onehot, upto, preferred_element_type=jnp.float32) + count
+        rank = jnp.sum(jnp.where(hit, upto_here, 0.0), axis=0, keepdims=True) - 1.0
+        rank = rank.astype(jnp.int32)
+        slot_vmem[pl.ds(c, 1), :] = dest * SLOTS + jnp.minimum(rank, KEPT)
+        part = jnp.where(high_half, jnp.right_shift(target, 5), jnp.bitwise_and(target, 31))
+        part = jnp.where(rank == rank_of_row, part, 0).astype(jnp.float32).astype(jnp.bfloat16)
+        labels = labels + lax.dot_general(
+            onehot, part, (((1,), (1,)), ((), ())), preferred_element_type=jnp.float32
+        )
+        return upto_here[:, LANES - 1 : LANES], labels
+
+    count = jnp.zeros((devices, 1), jnp.float32)
+    labels = jnp.zeros((devices, LANES), jnp.float32)
+    for c in range(chunks):
+        count, labels = rank_chunk(c, (count, labels))
+    copy = pltpu.make_async_copy(slot_vmem, slot_smem, sem)
+    copy.start()
+
+    def clear(n, carry):
+        out_ref[pl.ds(pl.multiple_of(n * 64, 64), 64), :] = jnp.zeros((64, LANES), jnp.float32)
+        return carry
+
+    lax.fori_loop(0, out_ref.shape[0] // 64, clear, 0)
+    most = jnp.max(count, axis=0, keepdims=True)
+    over = jnp.where(most > float(KEPT), 1.0, 0.0)
+    label_rows = labels * 32.0 + pltpu.roll(labels, 64, 1)
+    label_rows = jnp.where(cols < KEPT, label_rows, jnp.where(cols == FLAG_LANE, over, 0.0))
+    label_rows += angles_for_all(twiddle_ref, 0, FIRST_LANE)
+    label_rows += angles_for_all(twiddle_ref, 1, SECOND_LANE)
+    copy.wait()
+    per_row = LANES // UNROLL
+
+    def move(n, carry):
+        c = n // per_row
+        first = lax.rem(n, per_row) * UNROLL
+        base = pl.multiple_of(n * UNROLL, UNROLL)
+        for k in range(UNROLL):
+            out_ref[pl.ds(slot_smem[c, first + k], 1), :] = src_ref[pl.ds(base + k, 1), :]
+        return carry
+
+    lax.fori_loop(0, chunks * per_row, move, 0)
+    out_ref[pl.ds(KEPT, devices, stride=SLOTS), :] = label_rows
+
+
+def in_vmem(count):
+    return [pl.BlockSpec(memory_space=pltpu.VMEM)] * count
+
+
+def pack(owner, box, sources, twiddle):
+    count, width = sources.shape
+    chunks = count // LANES
+    return pl.pallas_call(
+        pack_kernel,
+        out_shape=jax.ShapeDtypeStruct((LANES * SLOTS, width), jnp.float32),
+        in_specs=in_vmem(4),
+        out_specs=in_vmem(1)[0],
+        scratch_shapes=[
+            pltpu.VMEM((chunks, LANES), jnp.int32),
+            pltpu.SMEM((chunks, LANES), jnp.int32),
+            pltpu.SemaphoreType.DMA,
+        ],
+        compiler_params=pltpu.CompilerParams(vmem_limit_bytes=VMEM_LIMIT),
+    )(owner.reshape(chunks, LANES), box.reshape(chunks, LANES), sources, twiddle)
+
+
+LAYOUTS = (
+    ("e0", "D1", "D2", "D4", "D5", "D3", "D6"),
+    ("e0", "e1", "D2", "D4", "D5", "D3", "D6"),
+    ("e0", "e1", "e2", "D4", "D5", "D3", "D6"),
+    ("D4", "D5", "e3", "e0", "e1", "e2", "D6"),
+    ("e4", "D5", "e3", "e0", "e1", "e2", "D6"),
+    ("e4", "e5", "e3", "e0", "e1", "e2", "D6"),
+    ("e4", "e5", "e6", "e0", "e1", "e2", "e3"),
+)
+MASKS = 0x1241124
+EXCHANGES_TO = 0x743
+
+
+def twiddle_place(level, position, device):
+    names = {}
+    for place, name in enumerate(LAYOUTS[level]):
+        names[name] = bit(position, 9 - place)
+    for b in range(3):
+        names["q" + str(b)] = bit(position, b)
+    owner = 0
+    for b in range(7):
+        here = names["D" + str(b)] if b > level else bit(device, b)
+        owner = owner + jnp.left_shift(here, b)
+    order = [bit(device, b) for b in range(level + 1, 7)]
+    order = order + [names["q2"], names["q1"], names["q0"]]
+    order = order + [names["e" + str(b)] for b in range(level + 1)]
+    index = 0
+    for value in order:
+        index = index * 2 + value
+    return owner, index
+
+
+def rotations(held, row, column, level, cos_ref, sin_ref):
+    pick = jnp.where(row == iota((held.shape[0], 8 * LANES), 0), 1.0, 0.0)
+    spread = exact_dot(held, pick, (0, 0))
+    mine = column == iota((LANES, 8 * LANES), 0)
+    angle = jnp.sum(jnp.where(mine, spread, 0.0), axis=0, keepdims=True)
+    angle = jnp.concatenate([angle[:, c * LANES : (c + 1) * LANES] for c in range(8)], axis=0)
+    cos_ref[level * 8 : level * 8 + 8, :] = jnp.cos(angle)
+    sin_ref[level * 8 : level * 8 + 8, :] = jnp.sin(angle)
+
+
+def split(value):
+    high = value.astype(jnp.bfloat16)
+    low = (value - high.astype(jnp.float32)).astype(jnp.bfloat16)
+    return high, low
+
+
+def prepare_kernel(
+    dev_ref, far_ref, twiddle_ref, leaf_ref, ops_ref,
+    cos_ref, sin_ref, leaf_h, leaf_l, mats_h, mats_l,
+):
+    device = dev_ref[0]
+    position = iota((1, 8 * LANES), 1)
+    cos_ref[0:16, :] = jnp.zeros((16, LANES), jnp.float32)
+    sin_ref[0:16, :] = jnp.zeros((16, LANES), jnp.float32)
+    for level in range(2, 7):
+        owner, index = twiddle_place(level, position, device)
+        column = jnp.bitwise_and(index, LANES - 1)
+        if level < 6:
+            row = jnp.bitwise_xor(jnp.right_shift(owner, 3), jnp.right_shift(device, 3))
+            kept = max(1, 2 ** (level - 3))
+            fixed = 0
+            for b in range(level + 1, min(7, level + 4)):
+                fixed = fixed * 2 + bit(device, b)
+            parts = []
+            for k in range(kept):
+                lane = pl.multiple_of((fixed * kept + k) * LANES, LANES)
+                parts.append(far_ref[:, pl.ds(lane, LANES)])
+            held = jnp.concatenate(parts, axis=0)
+            row = row * 4 + level - 2
+            row = row + far_ref.shape[0] * jnp.bitwise_and(jnp.right_shift(index, 7), kept - 1)
+        else:
+            held = jnp.concatenate(
+                [twiddle_ref[6:7, c * LANES : (c + 1) * LANES] for c in range(8)], axis=0
+            )
+            row = jnp.right_shift(index, 7)
+        rotations(held, row, column, level, cos_ref, sin_ref)
+
+    def block(real, imag):
+        top = jnp.concatenate([real, imag], axis=1)
+        bottom = jnp.concatenate([-imag, real], axis=1)
+        return jnp.concatenate([top, bottom], axis=0).T
+
+    leaf = block(leaf_ref[0], leaf_ref[1])
+    leaf_h[...], leaf_l[...] = split(leaf)
+
+    def build(n, carry):
+        level, e, c = n // 4, lax.rem(n, 4) // 2, lax.rem(n, 2)
+        high, low = split(block(ops_ref[level, e, c, 0], ops_ref[level, e, c, 1]))
+        out = pl.ds(pl.multiple_of(e * LANES, LANES), LANES)
+        across = pl.ds(pl.multiple_of(c * LANES, LANES), LANES)
+        mats_h[level, out, across] = high
+        mats_l[level, out, across] = low
+        return carry
+
+    lax.fori_loop(0, 4 * ops_ref.shape[0], build, 0, unroll=2)
+
+
+def prepare(twiddle, leaf_op, level_ops):
+    levels, count = twiddle.shape
+    width = 2 * leaf_op.shape[1]
+    device = lax.axis_index("gx") * lax.axis_size("gy") + lax.axis_index("gy")
+    far = twiddle[2:6]
+    for b in range(lax.axis_size("gx").bit_length() - 1):
+        far = jnp.concatenate([far, swapped(far, "gx", b)], axis=0)
+    return pl.pallas_call(
+        prepare_kernel,
+        out_shape=[
+            jax.ShapeDtypeStruct((levels * count // LANES, LANES), jnp.float32),
+            jax.ShapeDtypeStruct((levels * count // LANES, LANES), jnp.float32),
+            jax.ShapeDtypeStruct((width, width), jnp.bfloat16),
+            jax.ShapeDtypeStruct((width, width), jnp.bfloat16),
+            jax.ShapeDtypeStruct((levels, 2 * width, 2 * width), jnp.bfloat16),
+            jax.ShapeDtypeStruct((levels, 2 * width, 2 * width), jnp.bfloat16),
+        ],
+        in_specs=[pl.BlockSpec(memory_space=pltpu.SMEM)] + in_vmem(4),
+        out_specs=in_vmem(6),
+        compiler_params=pltpu.CompilerParams(vmem_limit_bytes=VMEM_LIMIT),
+    )(device.reshape(1).astype(jnp.int32), far, twiddle, leaf_op, level_ops)
+
+
+def product(high, low, value):
+    value_high, value_low = split(value)
+    total = jnp.dot(high, value_high, preferred_element_type=jnp.float32)
+    total += jnp.dot(high, value_low, preferred_element_type=jnp.float32)
+    total += jnp.dot(low, value_high, preferred_element_type=jnp.float32)
+    return total
+
+
+def nibble(table, n):
+    return jnp.bitwise_and(jnp.right_shift(table, 4 * n), 15)
+
+
+def finish_kernel(
+    dev_ref, x_ref, cos_in, sin_in, leaf_h, leaf_l, mats_h, mats_l,
+    out_ref, flag_ref, sums, names, state, cos_ref, sin_ref,
+):
+    devices = LANES
+    device = dev_ref[0]
+    half = LANES // 2
+    labels = x_ref[pl.ds(KEPT, devices, stride=SLOTS), :]
+    names[...] = labels.T - 1.0
+    flag_ref[0] = jnp.max(names[FLAG_LANE : FLAG_LANE + 1, :] + 1.0).astype(jnp.int32)
+    cos_ref[...] = cos_in[...]
+    sin_ref[...] = sin_in[...]
+    position = iota((1, 8 * LANES), 1)
+    for level, lane in ((0, FIRST_LANE), (1, SECOND_LANE)):
+        owner, index = twiddle_place(level, position, device)
+        column = lane + jnp.bitwise_and(index, (16 << level) - 1)
+        rotations(labels, owner, column, level, cos_ref, sin_ref)
+    targets = iota((8 * LANES, 2 * LANES), 0).astype(jnp.float32)
+    sums[...] = jnp.zeros_like(sums)
+
+    def gather(pair, carry):
+        rows = [x_ref[pl.ds(2 * pair + k, devices, stride=SLOTS), :] for k in range(2)]
+        name = [names[pl.ds(2 * pair + k, 1), :] for k in range(2)]
+        value = jnp.concatenate(rows, axis=0)
+        pick = jnp.where(targets == jnp.concatenate(name, axis=1), 1.0, 0.0).astype(jnp.bfloat16)
+        both = jnp.concatenate(split(value), axis=1)
+        sums[...] += jnp.dot(pick, both, preferred_element_type=jnp.float32)
+        return carry
+
+    lax.fori_loop(0, SLOTS // 2, gather, 0)
+
+    def leaf(c, carry):
+        block = sums[pl.ds(pl.multiple_of(c * LANES, LANES), LANES), :]
+        state[c] = product(leaf_h[...], leaf_l[...], (block[:, :LANES] + block[:, LANES:]).T)
+        return carry
+
+    lax.fori_loop(0, 8, leaf, 0)
+
+    def pairs(mask):
+        lows = [2 * n - jnp.bitwise_and(n, mask - 1) for n in range(4)]
+        return [(low, low + mask) for low in lows]
+
+    def level(number, carry):
+        mask = nibble(MASKS, number)
+        stacked = jnp.concatenate(
+            [
+                jnp.concatenate([state[pair[c]] for pair in pairs(mask)], axis=1)
+                for c in range(2)
+            ],
+            axis=0,
+        )
+        mixed = product(mats_h[number], mats_l[number], stacked)
+        for n, pair in enumerate(pairs(mask)):
+            for e in range(2):
+                block = mixed[e * LANES : (e + 1) * LANES, n * LANES : (n + 1) * LANES]
+                real, imag = block[:half], block[half:]
+                cosine = cos_ref[pl.ds(number * 8 + pair[e], 1), :]
+                sine = sin_ref[pl.ds(number * 8 + pair[e], 1), :]
+                state[pair[e], :half, :] = real * cosine - imag * sine
+                state[pair[e], half:, :] = real * sine + imag * cosine
+        return carry
+
+    def exchange(number, carry):
+        mask = nibble(MASKS, number)
+        weight = jnp.right_shift(half, number)
+        lane_set = jnp.bitwise_and(iota((LANES, LANES), 1), weight) != 0
+        for low, high in pairs(mask):
+            lower, upper = state[low], state[high]
+            state[low] = jnp.where(lane_set, pltpu.roll(upper, weight, 1), lower)
+            state[high] = jnp.where(lane_set, upper, pltpu.roll(lower, LANES - weight, 1))
+        return carry
+
+    def phase(number, done):
+        lax.fori_loop(3 * number, jnp.minimum(3 * number + 3, 7), level, 0)
+        then = nibble(EXCHANGES_TO, number)
+        lax.fori_loop(done, then, exchange, 0)
+        return then
+
+    lax.fori_loop(0, 3, phase, 0)
+
+    def write(c, carry):
+        out_ref[pl.ds(pl.multiple_of(c * LANES, LANES), LANES), :] = state[c].T
+        return carry
+
+    lax.fori_loop(0, 8, write, 0)
+
+
+def finish(arrived, prepared, box_count):
+    width = arrived.shape[1]
+    device = lax.axis_index("gx") * lax.axis_size("gy") + lax.axis_index("gy")
+    table = pltpu.VMEM(prepared[0].shape, jnp.float32)
+    return pl.pallas_call(
+        finish_kernel,
+        out_shape=[
+            jax.ShapeDtypeStruct((box_count, width), jnp.float32),
+            jax.ShapeDtypeStruct((1,), jnp.int32),
+        ],
+        in_specs=[pl.BlockSpec(memory_space=pltpu.SMEM)] + in_vmem(7),
+        out_specs=[
+            pl.BlockSpec(memory_space=pltpu.VMEM),
+            pl.BlockSpec(memory_space=pltpu.SMEM),
+        ],
+        scratch_shapes=[
+            pltpu.VMEM((box_count, 2 * width), jnp.float32),
+            pltpu.VMEM((LANES, LANES), jnp.float32),
+            pltpu.VMEM((8, width, LANES), jnp.float32),
+            table,
+            table,
+        ],
+        compiler_params=pltpu.CompilerParams(vmem_limit_bytes=VMEM_LIMIT),
+    )(device.reshape(1).astype(jnp.int32), arrived, *prepared)
+
+
+def local(sources, owner, box, leaf_op, level_ops, twiddle):
+    width = sources.shape[1]
+    box_count = twiddle.shape[1]
+    packed = pack(owner, box, sources, twiddle)
+    arrived = lax.all_to_all(
+        packed.reshape(-1, SLOTS, width), ("gx", "gy"), split_axis=0, concat_axis=0, tiled=True
+    ).reshape(-1, width)
+    prepared = prepare(twiddle, leaf_op, level_ops)
+    blocks, flag = finish(arrived, prepared, box_count)
+    return lax.cond(
+        flag[0] > 0,
+        lambda: general(sources, owner, box, leaf_op, level_ops, twiddle),
+        lambda: blocks,
+    )
+
+
 def solution(mesh):
     in_specs = (
         P(("gx", "gy"), None),

time: 160 us -> 92.1 us (0.58)
  the two profiles are of different devices: /device:TPU:1 before, /device:TPU:20 now
where the time goes in v1:
time: 92.1 us; the launch traced here: 91.7 us
  waiting for transfers between devices  39.5 us (43%)
  Pallas kernels  32 us (35%)
  starting transfers between devices  12.8 us (14%)
  local copies, waits for them, and re-layouts  6.5 us (7%)
    ppermute x4, waiting for transfers between devices, swapped(): lax.ppermute(shard, axis, [(i, i ^ 1 << stride) for i in range(lax.axis_s...  39.5 us
    pallas_call x1, Pallas kernels, finish(): pl.pallas_call(finish_kernel, out_shape=[jax.ShapeDtypeStruct((box_count,...  16.6 us
    all_to_all x1, starting transfers between devices, local(): lax.all_to_all(packed.reshape(-1, SLOTS, width), ('gx', 'gy'), split_axis...  10.3 us
    pallas_call x1, Pallas kernels, pack(): pl.pallas_call(pack_kernel, out_shape=jax.ShapeDtypeStruct((LANES * SLOTS...  8.58 us
    pallas_call x1, Pallas kernels, prepare(): pl.pallas_call(prepare_kernel, out_shape=[jax.ShapeDtypeStruct((levels *...  6.84 us
    unnamed x18, local copies, waits for them, and re-layouts  6.46 us
    ppermute x4, starting transfers between devices, swapped(): lax.ppermute(shard, axis, [(i, i ^ 1 << stride) for i in range(lax.axis_s...  2.47 us
  transfers between devices with their start and end apart: 5, of which 4 were waited for; matrix products, arithmetic and copies ran while one was open for 0% of the time, Pallas kernels for 7%

profile of v1, /device:TPU:20, one launch (start us, length us, event | category | flops | bytes accessed | tf_op | source)
XLA Modules:
  0.0 91.7 jit_solution(15505115680995616766)
XLA Ops:
  0.0 8.6 %shard_map.66 = f32[5120,128]{1,0:T(8,128)S(1)} custom-call(s32[16,128]{1,0:T(8,128)} %bitcast.225, s32[16,128]{1,0:T(8,128)} %bitcast.243, f32[2048,128]{1,0:T(8,128)} %src_ref.1, f32[7,1024]{1,0:T(8,128)} %twiddle_ref.3), custom_call_target="tpu_custom_call" | custom-call | tf_op jit(solution)/shard_map/pallas_call | solution.py:224
  8.6 0.0 copy-start
  8.6 1.5 %copy-done = f32[5120,128]{1,0:T(8,128)} copy-done((f32[5120,128]{1,0:T(8,128)}, f32[5120,128]{1,0:T(8,128)S(1)}, u32[]{:S(2)}) %copy-start) | copy-done | bytes 2621464
  10.1 0.0 copy-start.9
  10.1 0.0 copy-start.8
  10.1 10.3 %all-to-all-start.2 = ((f32[128,40,128]{2,1,0:T(8,128)}), f32[128,40,128]{2,1,0:T(8,128)S(1)}, u32[]{:S(2)}, u32[]{:S(2)}) async-start(f32[128,40,128]{2,1,0:T(8,128)} %bitcast.224), calls=%async_computation.2 | async-start | bytes 5242880 | tf_op jit(solution)/shard_map/all_to_all | solution.py:489
  20.4 0.0 copy-done.9
  20.4 0.2 collective-permute-start.7
  20.6 1.0 %collective-permute-done.7 = f32[4,1024]{1,0:T(4,128)S(1)} collective-permute-done((f32[4,1024]{1,0:T(4,128)S(1)}, f32[4,1024]{1,0:T(4,128)S(1)}, u32[]{:S(2)}, u32[]{:S(2)}) %collective-permute-start.7) | collective-permute-done | bytes 16416 | tf_op jit(solution)/shard_map/ppermute | solution.py:13
  21.7 1.8 %collective-permute-start.8 = (f32[8,1024]{1,0:T(8,128)S(1)}, f32[8,1024]{1,0:T(8,128)S(1)}, u32[]{:S(2)}, u32[]{:S(2)}) collective-permute-start(f32[8,1024]{1,0:T(8,128)S(1)} %pad_maximum_fusion.9), channel_id=1, source_target_pairs={{0,16},{8,24},{16,0},{24,8},{32,48},{40,56},{48,32},{56,40},{64,80... | collective-permute-start | bytes 98312 | tf_op jit(solution)/shard_map/ppermute | solution.py:13
  23.5 27.9 %collective-permute-done.8 = f32[8,1024]{1,0:T(8,128)S(1)} collective-permute-done((f32[8,1024]{1,0:T(8,128)S(1)}, f32[8,1024]{1,0:T(8,128)S(1)}, u32[]{:S(2)}, u32[]{:S(2)}) %collective-permute-start.8) | collective-permute-done | bytes 32800 | tf_op jit(solution)/shard_map/ppermute | solution.py:13
  51.4 0.3 collective-permute-start.9
  51.7 4.1 %collective-permute-done.9 = f32[16,1024]{1,0:T(8,128)S(1)} collective-permute-done((f32[16,1024]{1,0:T(8,128)S(1)}, f32[16,1024]{1,0:T(8,128)S(1)}, u32[]{:S(2)}, u32[]{:S(2)}) %collective-permute-start.9) | collective-permute-done | bytes 65568 | tf_op jit(solution)/shard_map/ppermute | solution.py:13
  55.9 0.1 collective-permute-start.10
  56.0 6.5 %collective-permute-done.10 = f32[32,1024]{1,0:T(8,128)S(1)} collective-permute-done((f32[32,1024]{1,0:T(8,128)S(1)}, f32[32,1024]{1,0:T(8,128)S(1)}, u32[]{:S(2)}, u32[]{:S(2)}) %collective-permute-start.10) | collective-permute-done | bytes 131104 | tf_op jit(solution)/shard_map/ppermute | solution.py:13
  62.5 0.0 copy-done.8
  62.5 6.8 %shard_map.67 = (f32[56,128]{1,0:T(8,128)S(1)}, f32[56,128]{1,0:T(8,128)S(1)}, bf16[128,128]{1,0:T(8,128)(2,1)S(1)}, bf16[128,128]{1,0:T(8,128)(2,1)S(1)}, bf16[...) custom-call(s32[1]{0:T(128)} %bitcast.89.dev_ref, f32[64,1024]{1,0:T(8,128)S(1)} %concatenate.384.far_ref, ...), custom_call_target="tpu_custom_call" | custom-call | tf_op jit(solution)/shard_map/pallas_call | solution.py:344
  69.3 0.0 copy-start.1
  69.3 0.9 copy-done.1
  70.3 0.0 copy-start.3
  70.3 0.9 %copy-done.3 = bf16[7,256,256]{2,1,0:T(8,128)(2,1)} copy-done((bf16[7,256,256]{2,1,0:T(8,128)(2,1)}, bf16[7,256,256]{2,1,0:T(8,128)(2,1)S(1)}, u32[]{:S(2)}) %copy-start.3) | copy-done | bytes 917528
  71.2 0.0 all-to-all-done.2
  71.2 0.0 copy-start.2
  71.2 1.2 %copy-done.2 = bf16[7,256,256]{2,1,0:T(8,128)(2,1)S(1)} copy-done((bf16[7,256,256]{2,1,0:T(8,128)(2,1)S(1)}, bf16[7,256,256]{2,1,0:T(8,128)(2,1)}, u32[]{:S(2)}) %copy-start.2) | copy-done | bytes 917528
  72.4 0.0 copy-start.4
  72.4 1.2 %copy-done.4 = bf16[7,256,256]{2,1,0:T(8,128)(2,1)S(1)} copy-done((bf16[7,256,256]{2,1,0:T(8,128)(2,1)S(1)}, bf16[7,256,256]{2,1,0:T(8,128)(2,1)}, u32[]{:S(2)}) %copy-start.4) | copy-done | bytes 917528
  73.5 0.0 copy-start.12
  73.5 16.6 %shard_map.68 = (f32[1024,128]{1,0:T(8,128)S(1)}, s32[1]{0:T(128)}) custom-call(s32[1]{0:T(128)} %bitcast.89.dev_ref, f32[5120,128]{1,0:T(8,128)S(1)} %bitcast.223, f32[56,128]{1,0:T(8,128)S(1)} %get-tuple-element.35.cos_in, f32[56,128]{1,0:T(8,128)S(1)} %get-tuple-element.36.sin_in, bf16[128,128]{1,0:T(8,128)(2,1)S(1)} %get-tuple-element.37.leaf_h, ...), custom_call_target="tpu_custom_call" | custom-call | tf_op jit(solution)/shard_map/pallas_call | solution.py:463
  90.7 0.0 copy-done.12
  90.7 0.2 conditional.1
  91.0 0.0 copy-start.21
  91.0 0.8 copy-done.21
  (5 shorter events, 0.1 us)
Async XLA Ops:
  8.6 1.5 %copy-start = (f32[5120,128]{1,0:T(8,128)}, f32[5120,128]{1,0:T(8,128)S(1)}, u32[]{:S(2)}) copy-start(f32[5120,128]{1,0:T(8,128)S(1)} %shard_map.66) | copy-start | bytes 7864324
  10.1 10.3 %copy-start.9 = (f32[7,1024]{1,0:T(8,128)S(1)}, f32[7,1024]{1,0:T(8,128)}, u32[]{:S(2)}) copy-start(f32[7,1024]{1,0:T(8,128)} %twiddle_ref.3) | copy-start | bytes 86020
  10.1 52.4 %copy-start.8 = (f32[2,64,64]{2,1,0:T(8,128)S(1)}, f32[2,64,64]{2,1,0:T(8,128)}, u32[]{:S(2)}) copy-start(f32[2,64,64]{2,1,0:T(8,128)} %leaf_ref.1) | copy-start | bytes 98308
  10.1 61.1 %all-to-all-start.2 = ((f32[128,40,128]{2,1,0:T(8,128)}), f32[128,40,128]{2,1,0:T(8,128)S(1)}, u32[]{:S(2)}, u32[]{:S(2)}) async-start(f32[128,40,128]{2,1,0:T(8,128)} %bitcast.224), calls=%async_computation.2 | async-start | bytes 5242880 | tf_op jit(solution)/shard_map/all_to_all | solution.py:489
  20.4 1.3 %collective-permute-start.7 = (f32[4,1024]{1,0:T(4,128)S(1)}, f32[4,1024]{1,0:T(4,128)S(1)}, u32[]{:S(2)}, u32[]{:S(2)}) collective-permute-start(f32[4,1024]{1,0:T(4,128)S(1)} %slice.480), channel_id=1, source_target_pairs={{0,8},{8,0},{16,24},{24,16},{32,40},{40,32},{48,56},{56,48},{64,72... | collective-permute-start | bytes 49160 | tf_op jit(solution)/shard_map/ppermute | solution.py:13
  21.7 29.7 %collective-permute-start.8 = (f32[8,1024]{1,0:T(8,128)S(1)}, f32[8,1024]{1,0:T(8,128)S(1)}, u32[]{:S(2)}, u32[]{:S(2)}) collective-permute-start(f32[8,1024]{1,0:T(8,128)S(1)} %pad_maximum_fusion.9), channel_id=1, source_target_pairs={{0,16},{8,24},{16,0},{24,8},{32,48},{40,56},{48,32},{56,40},{64,80... | collective-permute-start | bytes 98312 | tf_op jit(solution)/shard_map/ppermute | solution.py:13
  51.4 4.5 %collective-permute-start.9 = (f32[16,1024]{1,0:T(8,128)S(1)}, f32[16,1024]{1,0:T(8,128)S(1)}, u32[]{:S(2)}, u32[]{:S(2)}) collective-permute-start(f32[16,1024]{1,0:T(8,128)S(1)} %pad_maximum_fusion.8), channel_id=1, source_target_pairs={{0,32},{8,40},{16,48},{24,56},{32,0},{40,8},{48,16},{56,24},{64,96... | collective-permute-start | bytes 196616 | tf_op jit(solution)/shard_map/ppermute | solution.py:13
  55.9 6.6 %collective-permute-start.10 = (f32[32,1024]{1,0:T(8,128)S(1)}, f32[32,1024]{1,0:T(8,128)S(1)}, u32[]{:S(2)}, u32[]{:S(2)}) collective-permute-start(f32[32,1024]{1,0:T(8,128)S(1)} %pad_maximum_fusion.7), channel_id=1, source_target_pairs={{0,64},{8,72},{16,80},{24,88},{32,96},{40,104},{48,112},{56,120},{... | collective-permute-start | bytes 393224 | tf_op jit(solution)/shard_map/ppermute | solution.py:13
  69.3 0.9 %copy-start.1 = (bf16[7,256,256]{2,1,0:T(8,128)(2,1)}, bf16[7,256,256]{2,1,0:T(8,128)(2,1)S(1)}, u32[]{:S(2)}) copy-start(bf16[7,256,256]{2,1,0:T(8,128)(2,1)S(1)} %get-tuple-element.39.mats_h) | copy-start | bytes 2752516
  70.3 0.9 %copy-start.3 = (bf16[7,256,256]{2,1,0:T(8,128)(2,1)}, bf16[7,256,256]{2,1,0:T(8,128)(2,1)S(1)}, u32[]{:S(2)}) copy-start(bf16[7,256,256]{2,1,0:T(8,128)(2,1)S(1)} %get-tuple-element.40.mats_l) | copy-start | bytes 2752516
  71.2 1.2 %copy-start.2 = (bf16[7,256,256]{2,1,0:T(8,128)(2,1)S(1)}, bf16[7,256,256]{2,1,0:T(8,128)(2,1)}, u32[]{:S(2)}) copy-start(bf16[7,256,256]{2,1,0:T(8,128)(2,1)} %copy-done.1) | copy-start | bytes 2752516
  72.4 1.2 %copy-start.4 = (bf16[7,256,256]{2,1,0:T(8,128)(2,1)S(1)}, bf16[7,256,256]{2,1,0:T(8,128)(2,1)}, u32[]{:S(2)}) copy-start(bf16[7,256,256]{2,1,0:T(8,128)(2,1)} %copy-done.3) | copy-start | bytes 2752516
  73.5 17.2 %copy-start.12 = (s32[2048,1]{0,1:T(1,128)S(1)}, s32[2048,1]{0,1:T(1,128)}, u32[]{:S(2)}) copy-start(s32[2048,1]{0,1:T(1,128)} %param.9) | copy-start | bytes 24580
  91.0 0.8 copy-start.21

commit v2 on v1

v2 whole, which is shorter than its diff:
```python
import jax
import jax.numpy as jnp
from jax import lax
from jax.experimental import pallas as pl
from jax.experimental.pallas import tpu as pltpu
from jax.sharding import PartitionSpec as P

LANES = 128
VMEM_LIMIT = 48 * 1024 * 1024


def swapped(shard, axis, shift):
    return lax.ppermute(shard, axis, [(i, i ^ shift) for i in range(lax.axis_size(axis))])


SLOTS = 40
KEPT = SLOTS - 1
FLAG_LANE = 39
FIRST_LANE = 48
SECOND_LANE = 64
SURE = 16
STEP = 4


def bit(value, place):
    return jnp.bitwise_and(jnp.right_shift(value, place), 1)


def bits_to(value, places):
    total = None
    for source, target in places:
        term = jnp.left_shift(bit(value, source), target)
        total = term if total is None else total + term
    return total


def iota(shape, axis):
    return lax.broadcasted_iota(jnp.int32, shape, axis)


def exact_dot(left, right, contract=(1, 0)):
    return lax.dot_general(
        left,
        right,
        (((contract[0],), (contract[1],)), ((), ())),
        precision=lax.Precision.HIGHEST,
        preferred_element_type=jnp.float32,
    )


def angles_for_all(twiddle_ref, level, lane):
    width = 16 << level
    devices = LANES
    dest = iota((devices, LANES), 0)
    cols = iota((devices, LANES), 1)
    first = bits_to(dest, [(level + 1 + b, 2 - b) for b in range(3)])
    last = range(level + 4, 7)
    group = bits_to(dest, [(b, 6 - b) for b in last])
    rows = jnp.zeros((devices, LANES), jnp.float32)
    for g in range(8):
        part = twiddle_ref[level : level + 1, g * LANES : (g + 1) * LANES]
        rows = jnp.where(first == g, part, rows)
    rows = jnp.where(jnp.right_shift(cols, 4 + level) == group, rows, 0.0)
    fold = jnp.where(cols == lane + jnp.bitwise_and(dest, width - 1), 1.0, 0.0)
    return exact_dot(rows, fold)


def rank_kernel(
    round_ref, owner_hbm, box_hbm, twiddle_hbm, slot_ref, label_ref, owner_ref, box_ref, twiddle_ref, sems
):
    pairs = ((owner_hbm, owner_ref), (box_hbm, box_ref), (twiddle_hbm, twiddle_ref))
    copies = [pltpu.make_async_copy(a, b, sems.at[n]) for n, (a, b) in enumerate(pairs)]
    for copy in copies:
        copy.start()
    for copy in copies:
        copy.wait()
    chunks = owner_ref.shape[0]
    devices = LANES
    passed = round_ref[0] * KEPT
    rows = iota((devices, LANES), 0)
    cols = iota((devices, LANES), 1)
    upto = jnp.where(rows <= cols, 1.0, 0.0).astype(jnp.bfloat16)
    high_half = rows < 64
    rank_of_row = jnp.bitwise_and(rows, 63)
    owner = owner_ref[...]
    box = box_ref[...]
    dest = bits_to(box, [(3 + b, 6 - b) for b in range(7)])
    places = [(0, 9), (1, 8), (2, 7), (4, 6), (5, 5), (3, 4), (6, 3)]
    target = bits_to(owner, places) + jnp.bitwise_and(box, 7) + 1
    target_high = jnp.right_shift(target, 5)
    target_low = jnp.bitwise_and(target, 31)
    count = jnp.zeros((devices, 1), jnp.float32)
    labels = jnp.zeros((devices, LANES), jnp.float32)
    for c in range(chunks):
        dest_c = dest[c : c + 1, :]
        hit = dest_c == rows
        onehot = jnp.where(hit, 1.0, 0.0).astype(jnp.bfloat16)
        upto_here = jnp.dot(onehot, upto, preferred_element_type=jnp.float32) + count
        rank = jnp.sum(jnp.where(hit, upto_here, 0.0), axis=0, keepdims=True) - 1.0
        count = upto_here[:, LANES - 1 : LANES]
        rank = rank.astype(jnp.int32) - passed
        now = jnp.logical_and(rank >= 0, rank < KEPT)
        slot_ref[c : c + 1, :] = dest_c * SLOTS + jnp.where(now, rank, KEPT)
        part = jnp.where(high_half, target_high[c : c + 1, :], target_low[c : c + 1, :])
        part = jnp.where(rank == rank_of_row, part, 0).astype(jnp.float32).astype(jnp.bfloat16)
        labels = labels + lax.dot_general(
            onehot, part, (((1,), (1,)), ((), ())), preferred_element_type=jnp.float32
        )
    most = jnp.max(count, axis=0, keepdims=True)
    left = jnp.where(most > (passed + KEPT).astype(jnp.float32), 1.0, 0.0)
    label_rows = labels * 32.0 + pltpu.roll(labels, 64, 1)
    label_rows = jnp.where(cols < KEPT, label_rows, jnp.where(cols == FLAG_LANE, left, 0.0))
    label_rows += angles_for_all(twiddle_ref, 0, FIRST_LANE)
    label_rows += angles_for_all(twiddle_ref, 1, SECOND_LANE)
    label_ref[...] = label_rows


def move_kernel(slot_hbm, label_ref, src_ref, after_hbm, out_ref, slot_smem, sem):
    del after_hbm
    devices = LANES
    chunks = slot_smem.shape[0]
    slots = pltpu.make_async_copy(slot_hbm, slot_smem, sem)
    slots.start()

    def clear(n, carry):
        out_ref[pl.ds(pl.multiple_of(n * 64, 64), 64), :] = jnp.zeros((64, LANES), jnp.float32)
        return carry

    lax.fori_loop(0, out_ref.shape[0] // 64, clear, 0)
    slots.wait()

    def move(c, carry):
        base = pl.multiple_of(c * LANES, LANES)
        for k in range(LANES):
            out_ref[pl.ds(slot_smem[c, k], 1), :] = src_ref[pl.ds(base + k, 1), :]
        return carry

    lax.fori_loop(0, chunks, move, 0)
    out_ref[pl.ds(KEPT, devices, stride=SLOTS), :] = label_ref[...]


def params():
    return pltpu.CompilerParams(vmem_limit_bytes=VMEM_LIMIT)


def in_vmem(count):
    return [pl.BlockSpec(memory_space=pltpu.VMEM)] * count


def anywhere(count):
    return [pl.BlockSpec(memory_space=pl.ANY)] * count


def in_smem():
    return [pl.BlockSpec(memory_space=pltpu.SMEM)]


def rank(number, owner, box, twiddle):
    chunks = owner.shape[0] // LANES
    block = pltpu.VMEM((chunks, LANES), jnp.int32)
    return pl.pallas_call(
        rank_kernel,
        out_shape=[
            jax.ShapeDtypeStruct((chunks, LANES), jnp.int32),
            jax.ShapeDtypeStruct((LANES, LANES), jnp.float32),
        ],
        in_specs=in_smem() + anywhere(3),
        out_specs=in_vmem(2),
        scratch_shapes=[
            block,
            block,
            pltpu.VMEM(twiddle.shape, jnp.float32),
            pltpu.SemaphoreType.DMA((3,)),
        ],
        compiler_params=params(),
    )(number.reshape(1), owner.reshape(chunks, LANES), box.reshape(chunks, LANES), twiddle)


def move(slots, labels, sources, after):
    return pl.pallas_call(
        move_kernel,
        out_shape=jax.ShapeDtypeStruct((LANES * SLOTS, sources.shape[1]), jnp.float32),
        in_specs=anywhere(1) + in_vmem(2) + anywhere(1),
        out_specs=in_vmem(1)[0],
        scratch_shapes=[
            pltpu.SMEM(slots.shape, jnp.int32),
            pltpu.SemaphoreType.DMA,
        ],
        compiler_params=params(),
    )(slots, labels, sources, after)


def deliver(packed):
    width = packed.shape[1]
    return lax.all_to_all(
        packed.reshape(-1, SLOTS, width), ("gx", "gy"), split_axis=0, concat_axis=0, tiled=True
    ).reshape(-1, width)


LAYOUTS = (
    ("e0", "D1", "D2", "D4", "D5", "D3", "D6"),
    ("e0", "e1", "D2", "D4", "D5", "D3", "D6"),
    ("e0", "e1", "e2", "D4", "D5", "D3", "D6"),
    ("D4", "D5", "e3", "e0", "e1", "e2", "D6"),
    ("e4", "D5", "e3", "e0", "e1", "e2", "D6"),
    ("e4", "e5", "e3", "e0", "e1", "e2", "D6"),
    ("e4", "e5", "e6", "e0", "e1", "e2", "e3"),
)
MASKS = 0x1241124
EXCHANGES_TO = 0x743


def twiddle_place(level, position, device):
    names = {}
    for place, name in enumerate(LAYOUTS[level]):
        names[name] = bit(position, 9 - place)
    for b in range(3):
        names["q" + str(b)] = bit(position, b)
    owner = 0
    for b in range(7):
        here = names["D" + str(b)] if b > level else bit(device, b)
        owner = owner + jnp.left_shift(here, b)
    order = [bit(device, b) for b in range(level + 1, 7)]
    order = order + [names["q2"], names["q1"], names["q0"]]
    order = order + [names["e" + str(b)] for b in range(level + 1)]
    index = 0
    for value in order:
        index = index * 2 + value
    return owner, index


def rotations(held, row, column, level, cos_ref, sin_ref):
    pick = jnp.where(row == iota((held.shape[0], 8 * LANES), 0), 1.0, 0.0)
    spread = exact_dot(held, pick, (0, 0))
    mine = column == iota((LANES, 8 * LANES), 0)
    angle = jnp.sum(jnp.where(mine, spread, 0.0), axis=0, keepdims=True)
    angle = jnp.concatenate([angle[:, c * LANES : (c + 1) * LANES] for c in range(8)], axis=0)
    cos_ref[level * 8 : level * 8 + 8, :] = jnp.cos(angle)
    sin_ref[level * 8 : level * 8 + 8, :] = jnp.sin(angle)


def split(value):
    high = value.astype(jnp.bfloat16)
    low = (value - high.astype(jnp.float32)).astype(jnp.bfloat16)
    return high, low


def prepare_kernel(
    dev_ref, far0, far1, far2, far3, twiddle_ref, leaf_ref, ops_ref,
    cos_ref, sin_ref, leaf_h, leaf_l, mats_h, mats_l,
):
    device = dev_ref[0]
    position = iota((1, 8 * LANES), 1)
    cos_ref[0:16, :] = jnp.zeros((16, LANES), jnp.float32)
    sin_ref[0:16, :] = jnp.zeros((16, LANES), jnp.float32)
    for level in range(2, 7):
        owner, index = twiddle_place(level, position, device)
        column = jnp.bitwise_and(index, LANES - 1)
        if level < 6:
            row = jnp.bitwise_xor(jnp.right_shift(owner, 3), jnp.right_shift(device, 3))
            kept = max(1, 2 ** (level - 3))
            fixed = 0
            for b in range(level + 1, min(7, level + 4)):
                fixed = fixed * 2 + bit(device, b)
            parts = []
            for k in range(kept):
                lane = pl.multiple_of((fixed * kept + k) * LANES, LANES)
                parts += [far[:, pl.ds(lane, LANES)] for far in (far0, far1, far2, far3)]
            held = jnp.concatenate(parts, axis=0)
            close = jnp.bitwise_and(row, 3)
            if level == 2:
                place = jnp.where(close == 0, 0, jnp.where(close == 3, 7, 3 + close))
            elif level == 3:
                place = 1 + jnp.where(close == 2, 5, 0)
            else:
                place = level - 2
            row = jnp.right_shift(row, 2) * far0.shape[0] + place
            row = row + 4 * far0.shape[0] * jnp.bitwise_and(jnp.right_shift(index, 7), kept - 1)
        else:
            held = jnp.concatenate(
                [twiddle_ref[6:7, c * LANES : (c + 1) * LANES] for c in range(8)], axis=0
            )
            row = jnp.right_shift(index, 7)
        rotations(held, row, column, level, cos_ref, sin_ref)

    def block(real, imag):
        top = jnp.concatenate([real, imag], axis=1)
        bottom = jnp.concatenate([-imag, real], axis=1)
        return jnp.concatenate([top, bottom], axis=0).T

    leaf = block(leaf_ref[0], leaf_ref[1])
    leaf_h[...], leaf_l[...] = split(leaf)

    def build(n, carry):
        level, e, c = n // 4, lax.rem(n, 4) // 2, lax.rem(n, 2)
        high, low = split(block(ops_ref[level, e, c, 0], ops_ref[level, e, c, 1]))
        out = pl.ds(pl.multiple_of(e * LANES, LANES), LANES)
        across = pl.ds(pl.multiple_of(c * LANES, LANES), LANES)
        mats_h[level, out, across] = high
        mats_l[level, out, across] = low
        return carry

    lax.fori_loop(0, 4 * ops_ref.shape[0], build, 0, unroll=2)


def prepare(twiddle, far, leaf_op, level_ops):
    levels, count = twiddle.shape
    width = 2 * leaf_op.shape[1]
    return pl.pallas_call(
        prepare_kernel,
        out_shape=[
            jax.ShapeDtypeStruct((levels * count // LANES, LANES), jnp.float32),
            jax.ShapeDtypeStruct((levels * count // LANES, LANES), jnp.float32),
            jax.ShapeDtypeStruct((width, width), jnp.bfloat16),
            jax.ShapeDtypeStruct((width, width), jnp.bfloat16),
            jax.ShapeDtypeStruct((levels, 2 * width, 2 * width), jnp.bfloat16),
            jax.ShapeDtypeStruct((levels, 2 * width, 2 * width), jnp.bfloat16),
        ],
        in_specs=in_smem() + in_vmem(7),
        out_specs=in_vmem(6),
        compiler_params=params(),
    )(own_number(), *far, twiddle, leaf_op, level_ops)


def own_number():
    device = lax.axis_index("gx") * lax.axis_size("gy") + lax.axis_index("gy")
    return device.reshape(1).astype(jnp.int32)


def product(high, low, value):
    value_high, value_low = split(value)
    total = jnp.dot(high, value_high, preferred_element_type=jnp.float32)
    total += jnp.dot(high, value_low, preferred_element_type=jnp.float32)
    total += jnp.dot(low, value_high, preferred_element_type=jnp.float32)
    return total


def angle_rows(labels, device, cos_ref, sin_ref):
    position = iota((1, 8 * LANES), 1)
    for level, lane in ((0, FIRST_LANE), (1, SECOND_LANE)):
        owner, index = twiddle_place(level, position, device)
        column = lane + jnp.bitwise_and(index, (16 << level) - 1)
        rotations(labels, owner, column, level, cos_ref, sin_ref)


def add_rows(x_ref, names, first, count):
    ranks = [first + k for k in range(count)]
    value = jnp.concatenate([x_ref[pl.ds(r, LANES, stride=SLOTS), :] for r in ranks], axis=0)
    name = jnp.concatenate([names[pl.ds(r, 1), :] for r in ranks], axis=1)
    targets = iota((8 * LANES, count * LANES), 0).astype(jnp.float32)
    pick = jnp.where(targets == name, 1.0, 0.0).astype(jnp.bfloat16)
    both = jnp.concatenate(split(value), axis=1)
    return jnp.dot(pick, both, preferred_element_type=jnp.float32)


def chunk_pairs(mask):
    lows = [2 * n - (n & (mask - 1)) for n in range(4)]
    return [(low, low + mask) for low in lows]


def nibble(table, n):
    return (table >> (4 * n)) & 15


def exchange(state, mask, weight):
    lane_set = jnp.bitwise_and(iota((LANES, LANES), 1), weight) != 0
    out = list(state)
    for low, high in chunk_pairs(mask):
        lower, upper = state[low], state[high]
        out[low] = jnp.where(lane_set, pltpu.roll(upper, weight, 1), lower)
        out[high] = jnp.where(lane_set, upper, pltpu.roll(lower, LANES - weight, 1))
    return out


def butterfly(state, mask, high, low, cos_ref, sin_ref, number):
    half = LANES // 2
    stacked = jnp.concatenate(
        [jnp.concatenate([state[pair[c]] for pair in chunk_pairs(mask)], axis=1) for c in range(2)],
        axis=0,
    )
    mixed = product(high, low, stacked)
    out = list(state)
    for n, pair in enumerate(chunk_pairs(mask)):
        for e in range(2):
            block = mixed[e * LANES : (e + 1) * LANES, n * LANES : (n + 1) * LANES]
            real, imag = block[:half], block[half:]
            place = number * 8 + pair[e]
            cosine = cos_ref[place : place + 1, :]
            sine = sin_ref[place : place + 1, :]
            out[pair[e]] = jnp.concatenate(
                [real * cosine - imag * sine, real * sine + imag * cosine], axis=0
            )
    return out


def finish_kernel(
    dev_ref, x_ref, cos_in, sin_in, leaf_h_in, leaf_l_in, mats_h_in, mats_l_in,
    out_ref, flag_ref,
    sums, names, cos_ref, sin_ref, cos_far, sin_far, leaf_h, leaf_l, mats_h, mats_l, sems,
):
    pairs = (
        (cos_in, cos_far), (sin_in, sin_far), (leaf_h_in, leaf_h), (leaf_l_in, leaf_l),
        (mats_h_in, mats_h), (mats_l_in, mats_l),
    )
    copies = [pltpu.make_async_copy(a, b, sems.at[n]) for n, (a, b) in enumerate(pairs)]
    for copy in copies:
        copy.start()
    labels = x_ref[pl.ds(KEPT, LANES, stride=SLOTS), :]
    names[...] = labels.T - 1.0
    flag_ref[0] = jnp.max(names[FLAG_LANE : FLAG_LANE + 1, :] + 1.0).astype(jnp.int32)
    column = iota((LANES, LANES), 1)
    filled = jnp.logical_and(labels > 0.0, column < KEPT)
    most = jnp.max(jnp.where(filled, column + 1, 0).astype(jnp.float32)).astype(jnp.int32)
    sums[...] = add_rows(x_ref, names, 0, SURE)
    angle_rows(labels, dev_ref[0], cos_ref, sin_ref)
    for first in range(SURE, SLOTS, STEP):

        @pl.when(most > first)
        def _():
            sums[...] += add_rows(x_ref, names, first, STEP)

    for copy in copies:
        copy.wait()
    cos_ref[16:, :] = cos_far[16:, :]
    sin_ref[16:, :] = sin_far[16:, :]
    state = []
    for c in range(8):
        block = sums[c * LANES : (c + 1) * LANES, :]
        state.append((block[:, :LANES] + block[:, LANES:]).T)
    leafed = product(leaf_h[...], leaf_l[...], jnp.concatenate(state, axis=1))
    state = [leafed[:, c * LANES : (c + 1) * LANES] for c in range(8)]
    done = 0
    for number in range(7):
        mask = nibble(MASKS, number)
        state = butterfly(state, mask, mats_h[number], mats_l[number], cos_ref, sin_ref, number)
        if number in (2, 5, 6):
            then = nibble(EXCHANGES_TO, number // 3)
            for n in range(done, then):
                state = exchange(state, nibble(MASKS, n), LANES // 2 >> n)
            done = then
    for c in range(8):
        out_ref[c * LANES : (c + 1) * LANES, :] = state[c].T


def finish(arrived, prepared, box_count):
    width = arrived.shape[1]
    table = pltpu.VMEM(prepared[0].shape, jnp.float32)
    return pl.pallas_call(
        finish_kernel,
        out_shape=[
            jax.ShapeDtypeStruct((box_count, width), jnp.float32),
            jax.ShapeDtypeStruct((1,), jnp.int32),
        ],
        in_specs=in_smem() + in_vmem(1) + anywhere(6),
        out_specs=in_vmem(1) + in_smem(),
        scratch_shapes=[
            pltpu.VMEM((box_count, 2 * width), jnp.float32),
            pltpu.VMEM((LANES, LANES), jnp.float32),
            table,
            table,
        ]
        + [pltpu.VMEM(array.shape, array.dtype) for array in prepared]
        + [pltpu.SemaphoreType.DMA((len(prepared),))],
        compiler_params=params(),
    )(own_number(), arrived, *prepared)


def collect_kernel(x_ref, before_ref, sums, label_ref, flag_ref, names):
    labels = x_ref[pl.ds(KEPT, LANES, stride=SLOTS), :]
    label_ref[...] = labels
    names[...] = labels.T - 1.0
    flag_ref[0] = jnp.max(names[FLAG_LANE : FLAG_LANE + 1, :] + 1.0).astype(jnp.int32)
    names[FLAG_LANE : FLAG_LANE + 1, :] = jnp.full((1, LANES), -1.0)
    sums[...] = before_ref[...]

    def body(pair, carry):
        sums[...] += add_rows(x_ref, names, 2 * pair, 2)
        return carry

    lax.fori_loop(0, SLOTS // 2, body, 0)


def collect(arrived, sums):
    return pl.pallas_call(
        collect_kernel,
        out_shape=[
            jax.ShapeDtypeStruct(sums.shape, jnp.float32),
            jax.ShapeDtypeStruct((LANES, LANES), jnp.float32),
            jax.ShapeDtypeStruct((1,), jnp.int32),
        ],
        in_specs=in_vmem(2),
        out_specs=in_vmem(2) + in_smem(),
        scratch_shapes=[pltpu.VMEM((LANES, LANES), jnp.float32)],
        compiler_params=params(),
    )(arrived, sums)


def levels_kernel(
    dev_ref, sums, labels_ref, cos_in, sin_in, leaf_h, leaf_l, mats_h, mats_l,
    out_ref, state, cos_ref, sin_ref,
):
    half = LANES // 2
    cos_ref[...] = cos_in[...]
    sin_ref[...] = sin_in[...]
    angle_rows(labels_ref[...], dev_ref[0], cos_ref, sin_ref)

    def leaf(c, carry):
        block = sums[pl.ds(pl.multiple_of(c * LANES, LANES), LANES), :]
        state[c] = product(leaf_h[...], leaf_l[...], (block[:, :LANES] + block[:, LANES:]).T)
        return carry

    lax.fori_loop(0, 8, leaf, 0)

    def level(number, carry):
        pairs = chunk_pairs(nibble(MASKS, number))
        stacked = jnp.concatenate(
            [jnp.concatenate([state[pair[c]] for pair in pairs], axis=1) for c in range(2)], axis=0
        )
        mixed = product(mats_h[number], mats_l[number], stacked)
        for n, pair in enumerate(pairs):
            for e in range(2):
                block = mixed[e * LANES : (e + 1) * LANES, n * LANES : (n + 1) * LANES]
                real, imag = block[:half], block[half:]
                cosine = cos_ref[pl.ds(number * 8 + pair[e], 1), :]
                sine = sin_ref[pl.ds(number * 8 + pair[e], 1), :]
                state[pair[e], :half, :] = real * cosine - imag * sine
                state[pair[e], half:, :] = real * sine + imag * cosine
        return carry

    def swap(number, carry):
        weight = half >> number
        lane_set = jnp.bitwise_and(iota((LANES, LANES), 1), weight) != 0
        for low, high in chunk_pairs(nibble(MASKS, number)):
            lower, upper = state[low], state[high]
            state[low] = jnp.where(lane_set, pltpu.roll(upper, weight, 1), lower)
            state[high] = jnp.where(lane_set, upper, pltpu.roll(lower, LANES - weight, 1))
        return carry

    def phase(number, done):
        lax.fori_loop(3 * number, jnp.minimum(3 * number + 3, 7), level, 0)
        then = nibble(EXCHANGES_TO, number)
        lax.fori_loop(done, then, swap, 0)
        return then

    lax.fori_loop(0, 3, phase, 0)

    def write(c, carry):
        out_ref[pl.ds(pl.multiple_of(c * LANES, LANES), LANES), :] = state[c].T
        return carry

    lax.fori_loop(0, 8, write, 0)


def transform(sums, labels, prepared):
    box_count, width = sums.shape[0], sums.shape[1] // 2
    table = pltpu.VMEM(prepared[0].shape, jnp.float32)
    return pl.pallas_call(
        levels_kernel,
        out_shape=jax.ShapeDtypeStruct((box_count, width), jnp.float32),
        in_specs=in_smem() + in_vmem(8),
        out_specs=in_vmem(1)[0],
        scratch_shapes=[pltpu.VMEM((8, width, LANES), jnp.float32), table, table],
        compiler_params=params(),
    )(own_number(), sums, labels, *prepared)


def in_rounds(sources, owner, box, twiddle, prepared):
    box_count, width = twiddle.shape[1], sources.shape[1]

    def body(carry):
        number, sums, _, _ = carry
        slots, labels = rank(number, owner, box, twiddle)
        arrived = deliver(move(slots, labels, sources, labels))
        return (number + 1, *collect(arrived, sums))

    start = (
        jnp.int32(0),
        jnp.zeros((box_count, 2 * width), jnp.float32),
        jnp.zeros((LANES, LANES), jnp.float32),
        jnp.ones((1,), jnp.int32),
    )
    _, sums, labels, _ = lax.while_loop(lambda carry: carry[3][0] > 0, body, start)
    return transform(sums, labels, prepared)


def local(sources, owner, box, leaf_op, level_ops, twiddle):
    box_count = twiddle.shape[1]
    near = [swapped(twiddle, "gx", i) for i in (1, 2, 3)]
    slots, labels = rank(jnp.int32(0), owner, box, twiddle)
    slots, labels, *near = lax.optimization_barrier((slots, labels, *near))
    near = jnp.concatenate([twiddle[2:6], near[0][2:3], near[1][2:4], near[2][2:3]], axis=0)
    packed = move(slots, labels, sources, near)
    far = [near] + [swapped(near, "gx", i) for i in (4, 8, 12)]
    packed, *far = lax.optimization_barrier((packed, *far))
    arrived = deliver(packed)
    prepared = prepare(twiddle, far, leaf_op, level_ops)
    blocks, flag = finish(arrived, prepared, box_count)
    return lax.cond(
        flag[0] > 0,
        lambda: in_rounds(sources, owner, box, twiddle, prepared),
        lambda: blocks,
    )


def solution(mesh):
    in_specs = (
        P(("gx", "gy"), None),
        P(("gx", "gy"), None),
        P(("gx", "gy")),
        P(),
        P(),
        P(None, ("gx", "gy")),
    )
    out_specs = P(("gx", "gy"), None)
    return jax.shard_map(local, mesh=mesh, in_specs=in_specs, out_specs=out_specs, check_vma=False)
```

time: 92.1 us -> 71.9 us (0.78)
  the two profiles are of different devices: /device:TPU:20 before, /device:TPU:1 now
where the time goes in v2:
time: 71.9 us; the launch traced here: 71.5 us
  waiting for transfers between devices  27.9 us (39%)
  Pallas kernels  22.9 us (32%)
  starting transfers between devices  17.5 us (24%)
  local copies, waits for them, and re-layouts  2.3 us (3%)
  between operations  0.88 us (1%)
    all_to_all x1, waiting for transfers between devices, deliver(): lax.all_to_all(packed.reshape(-1, SLOTS, width), ('gx', 'gy'), split_axis...  27.9 us
    all_to_all x1, starting transfers between devices, deliver(): lax.all_to_all(packed.reshape(-1, SLOTS, width), ('gx', 'gy'), split_axis...  10.7 us
    pallas_call x1, Pallas kernels, finish(): pl.pallas_call(finish_kernel, out_shape=[jax.ShapeDtypeStruct((box_count,...  8.82 us
    ppermute x6, starting transfers between devices, swapped(): lax.ppermute(shard, axis, [(i, i ^ shift) for i in range(lax.axis_size(ax...  6.79 us
    pallas_call x1, Pallas kernels, prepare(): pl.pallas_call(prepare_kernel, out_shape=[jax.ShapeDtypeStruct((levels *...  6.42 us
    pallas_call x1, Pallas kernels, move(): pl.pallas_call(move_kernel, out_shape=jax.ShapeDtypeStruct((LANES * SLOTS...  5.12 us
    pallas_call x1, Pallas kernels, rank(): pl.pallas_call(rank_kernel, out_shape=[jax.ShapeDtypeStruct((chunks, LANE...  2.5 us
    unnamed x10, local copies, waits for them, and re-layouts  1.51 us
  transfers between devices with their start and end apart: 7, of which 1 were waited for; matrix products, arithmetic and copies ran while one was open for 1% of the time, Pallas kernels for 20%

profile of v2, /device:TPU:1, one launch (start us, length us, event | category | flops | bytes accessed | tf_op | source)
XLA Modules:
  0.0 71.5 jit_solution(7135937915123265098)
XLA Ops:
  0.0 3.0 %collective-permute-start.2 = (f32[7,1024]{1,0:T(8,128)}, f32[7,1024]{1,0:T(8,128)S(1)}, u32[]{:S(2)}, u32[]{:S(2)}) collective-permute-start(f32[7,1024]{1,0:T(8,128)} %twiddle_ref.1), channel_id=1, source_target_pairs={{0,24},{8,16},{16,8},{24,0},{32,56},{40,48},{48,40},{56,32},{64,88... | collective-permute-start | bytes 86024 | tf_op jit(solution)/shard_map/ppermute | solution.py:13
  3.0 0.0 collective-permute-start.1
  3.0 0.4 collective-permute-start
  3.5 0.8 %slice.12 = f32[4,1024]{1,0:T(4,128)S(1)} slice(f32[7,1024]{1,0:T(8,128)} %twiddle_ref.1), slice={[2:6], [0:1024]} | slice | bytes 32768 | tf_op jit(solution)/shard_map/slice | solution.py:591
  4.2 2.5 %shard_map.66 = (s32[16,128]{1,0:T(8,128)S(1)}, f32[128,128]{1,0:T(8,128)S(1)}) custom-call(s32[1]{0:T(128)} %constant.37.clone.1.round_ref, s32[16,128]{1,0:T(8,128)} %bitcast.27, s32[16,128]{1,0:T(8,128)} %bitcast.29, f32[7,1024]{1,0:T(8,128)} %twiddle_ref.1), custom_call_target="tpu_custom_call" | custom-call | tf_op jit(solution)/shard_map/pallas_call | solution.py:161
  6.7 0.0 collective-permute-done.2
  6.7 0.0 collective-permute-done.1
  6.8 0.0 collective-permute-done
  6.8 2.6 %collective-permute-start.5 = (f32[8,1024]{1,0:T(8,128)S(1)}, f32[8,1024]{1,0:T(8,128)S(1)}, u32[]{:S(2)}, u32[]{:S(2)}) collective-permute-start(f32[8,1024]{1,0:T(8,128)S(1)} %pad_maximum_fusion.after_hbm.far0), channel_id=1, source_target_pairs={{0,96},{8,104},{16,112},{24,120},{32,64},{40,72},{48,80},{56,88},{... | collective-permute-start | bytes 98312 | tf_op jit(solution)/shard_map/ppermute | solution.py:13
  9.4 0.5 collective-permute-start.4
  9.9 0.3 collective-permute-start.3
  10.2 5.1 %shard_map.67 = f32[5120,128]{1,0:T(8,128)} custom-call(s32[16,128]{1,0:T(8,128)S(1)} %get-tuple-element.107.slot_hbm, f32[128,128]{1,0:T(8,128)S(1)} %get-tuple-element.108.label_ref, f32[2048,128]{1,0:T(8,128)} %src_ref.1, f32[8,1024]{1,0:T(8,128)S(1)} %pad_maximum_fusion.after_hbm.far0), custom_call_target="tpu_custom_call" | custom-call | tf_op jit(solution)/shard_map/pallas_call | solution.py:180
  15.3 0.0 collective-permute-done.5.far3
  15.3 0.0 collective-permute-done.4.far2
  15.3 0.0 collective-permute-done.3.far1
  15.3 0.0 copy-start.3
  15.3 0.0 copy-start.5
  15.4 10.7 %all-to-all-start.1 = ((f32[128,40,128]{2,1,0:T(8,128)}), f32[128,40,128]{2,1,0:T(8,128)S(1)}, u32[]{:S(2)}, u32[]{:S(2)}) async-start(f32[128,40,128]{2,1,0:T(8,128)} %bitcast.10), calls=%async_computation.1 | async-start | bytes 5242880 | tf_op jit(solution)/shard_map/all_to_all | solution.py:195
  26.1 0.0 copy-done.3
  26.1 0.0 copy-done.5
  26.1 0.0 copy-start.2
  26.1 1.5 %copy-done.2 = f32[7,2,2,2,64,64]{5,4,3,2,1,0:T(8,128)S(1)} copy-done((f32[7,2,2,2,64,64]{5,4,3,2,1,0:T(8,128)S(1)}, f32[7,2,2,2,64,64]{5,4,3,2,1,0:T(8,128)}, u32[]{:S(2)}) %copy-start.2) | copy-done | bytes 917528
  27.6 6.4 %shard_map.68 = (f32[56,128]{1,0:T(8,128)S(1)}, f32[56,128]{1,0:T(8,128)S(1)}, bf16[128,128]{1,0:T(8,128)(2,1)S(1)}, bf16[128,128]{1,0:T(8,128)(2,1)S(1)}, bf16[...) custom-call(s32[1]{0:T(128)} %bitcast.7.dev_ref, f32[8,1024]{1,0:T(8,128)S(1)} %pad_maximum_fusion.after_hbm.far0, ...), custom_call_target="tpu_custom_call" | custom-call | tf_op jit(solution)/shard_map/pallas_call | solution.py:309
  34.1 0.0 copy-start.7
  34.1 0.0 copy-start.8
  34.1 27.9 %all-to-all-done.1 = f32[128,40,128]{2,1,0:T(8,128)S(1)} async-done(((f32[128,40,128]{2,1,0:T(8,128)}), f32[128,40,128]{2,1,0:T(8,128)S(1)}, u32[]{:S(2)}, u32[]{:S(2)}) %all-to-all-start.1) | async-done | bytes 2621472 | tf_op jit(solution)/shard_map/all_to_all | solution.py:195
  61.9 8.8 %shard_map.69 = (f32[1024,128]{1,0:T(8,128)}, s32[1]{0:T(128)}) custom-call(s32[1]{0:T(128)} %bitcast.7.dev_ref, f32[5120,128]{1,0:T(8,128)S(1)} %bitcast.26, f32[56,128]{1,0:T(8,128)S(1)} %get-tuple-element.117.cos_in, f32[56,128]{1,0:T(8,128)S(1)} %get-tuple-element.118.sin_in, bf16[128,128]{1,0:T(8,128)(2,1)S(1)} %get-tuple-element.119.leaf_h_in, ...), custom_call_target="tpu_custom_call" | custom-call | tf_op jit(solution)/shard_map/pallas_call | solution.py:448
  71.3 0.0 copy-done.7
  71.3 0.0 copy-done.8
  (5 shorter events, 0.0 us)
Async XLA Ops:
  0.0 6.7 %collective-permute-start.2 = (f32[7,1024]{1,0:T(8,128)}, f32[7,1024]{1,0:T(8,128)S(1)}, u32[]{:S(2)}, u32[]{:S(2)}) collective-permute-start(f32[7,1024]{1,0:T(8,128)} %twiddle_ref.1), channel_id=1, source_target_pairs={{0,24},{8,16},{16,8},{24,0},{32,56},{40,48},{48,40},{56,32},{64,88... | collective-permute-start | bytes 86024 | tf_op jit(solution)/shard_map/ppermute | solution.py:13
  3.0 3.7 %collective-permute-start.1 = (f32[7,1024]{1,0:T(8,128)}, f32[7,1024]{1,0:T(8,128)S(1)}, u32[]{:S(2)}, u32[]{:S(2)}) collective-permute-start(f32[7,1024]{1,0:T(8,128)} %twiddle_ref.1), channel_id=1, source_target_pairs={{0,16},{8,24},{16,0},{24,8},{32,48},{40,56},{48,32},{56,40},{64,80... | collective-permute-start | bytes 86024 | tf_op jit(solution)/shard_map/ppermute | solution.py:13
  3.0 3.7 %collective-permute-start = (f32[7,1024]{1,0:T(8,128)}, f32[7,1024]{1,0:T(8,128)S(1)}, u32[]{:S(2)}, u32[]{:S(2)}) collective-permute-start(f32[7,1024]{1,0:T(8,128)} %twiddle_ref.1), channel_id=1, source_target_pairs={{0,8},{8,0},{16,24},{24,16},{32,40},{40,32},{48,56},{56,48},{64,72... | collective-permute-start | bytes 86024 | tf_op jit(solution)/shard_map/ppermute | solution.py:13
  6.8 8.5 %collective-permute-start.5 = (f32[8,1024]{1,0:T(8,128)S(1)}, f32[8,1024]{1,0:T(8,128)S(1)}, u32[]{:S(2)}, u32[]{:S(2)}) collective-permute-start(f32[8,1024]{1,0:T(8,128)S(1)} %pad_maximum_fusion.after_hbm.far0), channel_id=1, source_target_pairs={{0,96},{8,104},{16,112},{24,120},{32,64},{40,72},{48,80},{56,88},{... | collective-permute-start | bytes 98312 | tf_op jit(solution)/shard_map/ppermute | solution.py:13
  9.4 5.9 %collective-permute-start.4 = (f32[8,1024]{1,0:T(8,128)S(1)}, f32[8,1024]{1,0:T(8,128)S(1)}, u32[]{:S(2)}, u32[]{:S(2)}) collective-permute-start(f32[8,1024]{1,0:T(8,128)S(1)} %pad_maximum_fusion.after_hbm.far0), channel_id=1, source_target_pairs={{0,64},{8,72},{16,80},{24,88},{32,96},{40,104},{48,112},{56,120},{... | collective-permute-start | bytes 98312 | tf_op jit(solution)/shard_map/ppermute | solution.py:13
  9.9 5.4 %collective-permute-start.3 = (f32[8,1024]{1,0:T(8,128)S(1)}, f32[8,1024]{1,0:T(8,128)S(1)}, u32[]{:S(2)}, u32[]{:S(2)}) collective-permute-start(f32[8,1024]{1,0:T(8,128)S(1)} %pad_maximum_fusion.after_hbm.far0), channel_id=1, source_target_pairs={{0,32},{8,40},{16,48},{24,56},{32,0},{40,8},{48,16},{56,24},{64,96... | collective-permute-start | bytes 98312 | tf_op jit(solution)/shard_map/ppermute | solution.py:13
  15.3 10.8 %copy-start.3 = (f32[2,64,64]{2,1,0:T(8,128)S(1)}, f32[2,64,64]{2,1,0:T(8,128)}, u32[]{:S(2)}) copy-start(f32[2,64,64]{2,1,0:T(8,128)} %leaf_ref.1) | copy-start | bytes 98308
  15.3 10.8 %copy-start.5 = (f32[7,1024]{1,0:T(8,128)S(1)}, f32[7,1024]{1,0:T(8,128)}, u32[]{:S(2)}) copy-start(f32[7,1024]{1,0:T(8,128)} %twiddle_ref.1) | copy-start | bytes 86020
  15.4 46.6 %all-to-all-start.1 = ((f32[128,40,128]{2,1,0:T(8,128)}), f32[128,40,128]{2,1,0:T(8,128)S(1)}, u32[]{:S(2)}, u32[]{:S(2)}) async-start(f32[128,40,128]{2,1,0:T(8,128)} %bitcast.10), calls=%async_computation.1 | async-start | bytes 5242880 | tf_op jit(solution)/shard_map/all_to_all | solution.py:195
  26.1 1.5 %copy-start.2 = (f32[7,2,2,2,64,64]{5,4,3,2,1,0:T(8,128)S(1)}, f32[7,2,2,2,64,64]{5,4,3,2,1,0:T(8,128)}, u32[]{:S(2)}) copy-start(f32[7,2,2,2,64,64]{5,4,3,2,1,0:T(8,128)} %ops_ref.1) | copy-start | bytes 2752516
  34.1 37.3 %copy-start.7 = (s32[2048,1]{0,1:T(1,128)S(1)}, s32[2048,1]{0,1:T(1,128)}, u32[]{:S(2)}) copy-start(s32[2048,1]{0,1:T(1,128)} %param.11) | copy-start | bytes 24580
  34.1 37.3 %copy-start.8 = (s32[2048]{0:T(1024)S(1)}, s32[2048]{0:T(1024)}, u32[]{:S(2)}) copy-start(s32[2048]{0:T(1024)} %param.12) | copy-start | bytes 24580

commit v3 on v2

--- a/solution.py
+++ b/solution.py
@@ -14,10 +14,12 @@
 
 
 SLOTS = 40
-KEPT = SLOTS - 1
-FLAG_LANE = 39
-FIRST_LANE = 48
-SECOND_LANE = 64
+KEPT = SLOTS - 2
+LABEL_ROW = KEPT
+FLAG_LANE = KEPT
+ANGLE_ROW = KEPT + 1
+ANGLE_LANES = (0, 32, 64)
+THIRD_ROW = KEPT - 1
 SURE = 16
 STEP = 4
 
@@ -65,18 +67,33 @@
     return exact_dot(rows, fold)
 
 
-def rank_kernel(
-    round_ref, owner_hbm, box_hbm, twiddle_hbm, slot_ref, label_ref, owner_ref, box_ref, twiddle_ref, sems
+def pack_kernel(
+    round_ref, dev_ref, owner_hbm, box_hbm, twiddle_hbm, src_hbm, out_ref,
+    owner_ref, box_ref, twiddle_ref, src_ref, slot_vmem, slot_smem, sems,
 ):
-    pairs = ((owner_hbm, owner_ref), (box_hbm, box_ref), (twiddle_hbm, twiddle_ref))
+    pairs = (
+        (owner_hbm, owner_ref), (box_hbm, box_ref), (twiddle_hbm, twiddle_ref), (src_hbm, src_ref),
+        (slot_vmem, slot_smem),
+    )
     copies = [pltpu.make_async_copy(a, b, sems.at[n]) for n, (a, b) in enumerate(pairs)]
-    for copy in copies:
+    for copy in copies[:4]:
         copy.start()
-    for copy in copies:
-        copy.wait()
+
+    def clear(n, carry):
+        out_ref[pl.ds(pl.multiple_of(n * 64, 64), 64), :] = jnp.zeros((64, LANES), jnp.float32)
+        return carry
+
+    lax.fori_loop(0, out_ref.shape[0] // 64, clear, 0)
+    copies[0].wait()
+    copies[1].wait()
     chunks = owner_ref.shape[0]
     devices = LANES
-    passed = round_ref[0] * KEPT
+    number, device = round_ref[0], dev_ref[0]
+
+    def kept(dest):
+        shared = jnp.bitwise_and(jnp.bitwise_xor(dest, device), 15) == 0
+        return jnp.where(shared, THIRD_ROW, KEPT)
+
     rows = iota((devices, LANES), 0)
     cols = iota((devices, LANES), 1)
     upto = jnp.where(rows <= cols, 1.0, 0.0).astype(jnp.bfloat16)
@@ -98,36 +115,25 @@
         upto_here = jnp.dot(onehot, upto, preferred_element_type=jnp.float32) + count
         rank = jnp.sum(jnp.where(hit, upto_here, 0.0), axis=0, keepdims=True) - 1.0
         count = upto_here[:, LANES - 1 : LANES]
-        rank = rank.astype(jnp.int32) - passed
-        now = jnp.logical_and(rank >= 0, rank < KEPT)
-        slot_ref[c : c + 1, :] = dest_c * SLOTS + jnp.where(now, rank, KEPT)
+        kept_c = kept(dest_c)
+        rank = rank.astype(jnp.int32) - number * kept_c
+        now = jnp.logical_and(rank >= 0, rank < kept_c)
+        slot_vmem[c : c + 1, :] = dest_c * SLOTS + jnp.where(now, rank, LABEL_ROW)
         part = jnp.where(high_half, target_high[c : c + 1, :], target_low[c : c + 1, :])
         part = jnp.where(rank == rank_of_row, part, 0).astype(jnp.float32).astype(jnp.bfloat16)
         labels = labels + lax.dot_general(
             onehot, part, (((1,), (1,)), ((), ())), preferred_element_type=jnp.float32
         )
-    most = jnp.max(count, axis=0, keepdims=True)
-    left = jnp.where(most > (passed + KEPT).astype(jnp.float32), 1.0, 0.0)
+    copies[4].start()
+    copies[2].wait()
+    angle_rows = sum(angles_for_all(twiddle_ref, n, lane) for n, lane in enumerate(ANGLE_LANES))
+    passes = kept(rows)
+    most = jnp.max(count - ((number + 1) * passes[:, :1]).astype(jnp.float32), axis=0, keepdims=True)
+    left = jnp.where(most > 0.0, 1.0, 0.0)
     label_rows = labels * 32.0 + pltpu.roll(labels, 64, 1)
-    label_rows = jnp.where(cols < KEPT, label_rows, jnp.where(cols == FLAG_LANE, left, 0.0))
-    label_rows += angles_for_all(twiddle_ref, 0, FIRST_LANE)
-    label_rows += angles_for_all(twiddle_ref, 1, SECOND_LANE)
-    label_ref[...] = label_rows
-
-
-def move_kernel(slot_hbm, label_ref, src_ref, after_hbm, out_ref, slot_smem, sem):
-    del after_hbm
-    devices = LANES
-    chunks = slot_smem.shape[0]
-    slots = pltpu.make_async_copy(slot_hbm, slot_smem, sem)
-    slots.start()
-
-    def clear(n, carry):
-        out_ref[pl.ds(pl.multiple_of(n * 64, 64), 64), :] = jnp.zeros((64, LANES), jnp.float32)
-        return carry
-
-    lax.fori_loop(0, out_ref.shape[0] // 64, clear, 0)
-    slots.wait()
+    label_rows = jnp.where(cols < passes, label_rows, jnp.where(cols == FLAG_LANE, left, 0.0))
+    copies[4].wait()
+    copies[3].wait()
 
     def move(c, carry):
         base = pl.multiple_of(c * LANES, LANES)
@@ -136,7 +142,17 @@
         return carry
 
     lax.fori_loop(0, chunks, move, 0)
-    out_ref[pl.ds(KEPT, devices, stride=SLOTS), :] = label_ref[...]
+    out_ref[pl.ds(LABEL_ROW, devices, stride=SLOTS), :] = label_rows
+    out_ref[pl.ds(ANGLE_ROW, devices, stride=SLOTS), :] = angle_rows
+    for h in range(8):
+        part = 4 * (h & 1) + (h & 2) + (h >> 2)
+        out_ref[pl.ds(third_place(device, h), 1), :] = twiddle_ref[
+            3:4, part * LANES : (part + 1) * LANES
+        ]
+
+
+def third_place(device, h):
+    return ((device & 15) + 16 * h) * SLOTS + THIRD_ROW
 
 
 def params():
@@ -155,39 +171,33 @@
     return [pl.BlockSpec(memory_space=pltpu.SMEM)]
 
 
-def rank(number, owner, box, twiddle):
-    chunks = owner.shape[0] // LANES
+def pack(number, sources, owner, box, twiddle):
+    count, width = sources.shape
+    chunks = count // LANES
     block = pltpu.VMEM((chunks, LANES), jnp.int32)
     return pl.pallas_call(
-        rank_kernel,
-        out_shape=[
-            jax.ShapeDtypeStruct((chunks, LANES), jnp.int32),
-            jax.ShapeDtypeStruct((LANES, LANES), jnp.float32),
-        ],
-        in_specs=in_smem() + anywhere(3),
-        out_specs=in_vmem(2),
+        pack_kernel,
+        out_shape=jax.ShapeDtypeStruct((LANES * SLOTS, width), jnp.float32),
+        in_specs=in_smem() * 2 + anywhere(4),
+        out_specs=in_vmem(1)[0],
         scratch_shapes=[
             block,
             block,
             pltpu.VMEM(twiddle.shape, jnp.float32),
-            pltpu.SemaphoreType.DMA((3,)),
+            pltpu.VMEM(sources.shape, jnp.float32),
+            block,
+            pltpu.SMEM((chunks, LANES), jnp.int32),
+            pltpu.SemaphoreType.DMA((5,)),
         ],
         compiler_params=params(),
-    )(number.reshape(1), owner.reshape(chunks, LANES), box.reshape(chunks, LANES), twiddle)
-
-
-def move(slots, labels, sources, after):
-    return pl.pallas_call(
-        move_kernel,
-        out_shape=jax.ShapeDtypeStruct((LANES * SLOTS, sources.shape[1]), jnp.float32),
-        in_specs=anywhere(1) + in_vmem(2) + anywhere(1),
-        out_specs=in_vmem(1)[0],
-        scratch_shapes=[
-            pltpu.SMEM(slots.shape, jnp.int32),
-            pltpu.SemaphoreType.DMA,
-        ],
-        compiler_params=params(),
-    )(slots, labels, sources, after)
+    )(
+        number.reshape(1),
+        own_number(),
+        owner.reshape(chunks, LANES),
+        box.reshape(chunks, LANES),
+        twiddle,
+        sources,
+    )
 
 
 def deliver(packed):
@@ -246,42 +256,14 @@
 
 
 def prepare_kernel(
-    dev_ref, far0, far1, far2, far3, twiddle_ref, leaf_ref, ops_ref,
-    cos_ref, sin_ref, leaf_h, leaf_l, mats_h, mats_l,
+    dev_ref, twiddle_ref, leaf_ref, ops_ref, cos_ref, sin_ref, leaf_h, leaf_l, mats_h, mats_l
 ):
-    device = dev_ref[0]
-    position = iota((1, 8 * LANES), 1)
-    cos_ref[0:16, :] = jnp.zeros((16, LANES), jnp.float32)
-    sin_ref[0:16, :] = jnp.zeros((16, LANES), jnp.float32)
-    for level in range(2, 7):
-        owner, index = twiddle_place(level, position, device)
-        column = jnp.bitwise_and(index, LANES - 1)
-        if level < 6:
-            row = jnp.bitwise_xor(jnp.right_shift(owner, 3), jnp.right_shift(device, 3))
-            kept = max(1, 2 ** (level - 3))
-            fixed = 0
-            for b in range(level + 1, min(7, level + 4)):
-                fixed = fixed * 2 + bit(device, b)
-            parts = []
-            for k in range(kept):
-                lane = pl.multiple_of((fixed * kept + k) * LANES, LANES)
-                parts += [far[:, pl.ds(lane, LANES)] for far in (far0, far1, far2, far3)]
-            held = jnp.concatenate(parts, axis=0)
-            close = jnp.bitwise_and(row, 3)
-            if level == 2:
-                place = jnp.where(close == 0, 0, jnp.where(close == 3, 7, 3 + close))
-            elif level == 3:
-                place = 1 + jnp.where(close == 2, 5, 0)
-            else:
-                place = level - 2
-            row = jnp.right_shift(row, 2) * far0.shape[0] + place
-            row = row + 4 * far0.shape[0] * jnp.bitwise_and(jnp.right_shift(index, 7), kept - 1)
-        else:
-            held = jnp.concatenate(
-                [twiddle_ref[6:7, c * LANES : (c + 1) * LANES] for c in range(8)], axis=0
-            )
-            row = jnp.right_shift(index, 7)
-        rotations(held, row, column, level, cos_ref, sin_ref)
+    cos_ref[0:48, :] = jnp.zeros((48, LANES), jnp.float32)
+    sin_ref[0:48, :] = jnp.zeros((48, LANES), jnp.float32)
+    _, index = twiddle_place(6, iota((1, 8 * LANES), 1), dev_ref[0])
+    angles = [twiddle_ref[6:7, c * LANES : (c + 1) * LANES] for c in range(8)]
+    row, column = jnp.right_shift(index, 7), jnp.bitwise_and(index, LANES - 1)
+    rotations(jnp.concatenate(angles, axis=0), row, column, 6, cos_ref, sin_ref)
 
     def block(real, imag):
         top = jnp.concatenate([real, imag], axis=1)
@@ -303,7 +285,7 @@
     lax.fori_loop(0, 4 * ops_ref.shape[0], build, 0, unroll=2)
 
 
-def prepare(twiddle, far, leaf_op, level_ops):
+def prepare(twiddle, leaf_op, level_ops):
     levels, count = twiddle.shape
     width = 2 * leaf_op.shape[1]
     return pl.pallas_call(
@@ -316,10 +298,10 @@
             jax.ShapeDtypeStruct((levels, 2 * width, 2 * width), jnp.bfloat16),
             jax.ShapeDtypeStruct((levels, 2 * width, 2 * width), jnp.bfloat16),
         ],
-        in_specs=in_smem() + in_vmem(7),
+        in_specs=in_smem() + in_vmem(3),
         out_specs=in_vmem(6),
         compiler_params=params(),
-    )(own_number(), *far, twiddle, leaf_op, level_ops)
+    )(own_number(), twiddle, leaf_op, level_ops)
 
 
 def own_number():
@@ -335,12 +317,35 @@
     return total
 
 
-def angle_rows(labels, device, cos_ref, sin_ref):
+def moved_rotations(angles, third, peers, device, cos_ref, sin_ref):
     position = iota((1, 8 * LANES), 1)
-    for level, lane in ((0, FIRST_LANE), (1, SECOND_LANE)):
+    for level in range(6):
         owner, index = twiddle_place(level, position, device)
-        column = lane + jnp.bitwise_and(index, (16 << level) - 1)
-        rotations(labels, owner, column, level, cos_ref, sin_ref)
+        if level < 3:
+            held, row = angles, owner
+            column = ANGLE_LANES[level] + jnp.bitwise_and(index, (16 << level) - 1)
+        elif level == 3:
+            held, row = third, jnp.right_shift(owner, 4)
+            column = jnp.bitwise_and(index, LANES - 1)
+        else:
+            taken = 2 ** (level - 3)
+            fixed = 0
+            for b in range(level + 1, 7):
+                fixed = fixed * 2 + bit(device, b)
+            parts = []
+            for k in range(taken):
+                lane = pl.multiple_of((fixed * taken + k) * LANES, LANES)
+                parts += [peer[level : level + 1, pl.ds(lane, LANES)] for peer in peers]
+            held = jnp.concatenate(parts, axis=0)
+            row = jnp.right_shift(jnp.bitwise_xor(owner, device), 5)
+            row = row + 4 * jnp.bitwise_and(jnp.right_shift(index, 7), taken - 1)
+            column = jnp.bitwise_and(index, LANES - 1)
+        rotations(held, row, column, level, cos_ref, sin_ref)
+
+
+def third_angles(x_ref, device):
+    rows = [x_ref[pl.ds(third_place(device, h), 1), :] for h in range(8)]
+    return jnp.concatenate(rows, axis=0)
 
 
 def add_rows(x_ref, names, first, count):
@@ -394,8 +399,8 @@
 
 
 def finish_kernel(
-    dev_ref, x_ref, cos_in, sin_in, leaf_h_in, leaf_l_in, mats_h_in, mats_l_in,
-    out_ref, flag_ref,
+    dev_ref, x_ref, peer0, peer1, peer2, peer3,
+    cos_in, sin_in, leaf_h_in, leaf_l_in, mats_h_in, mats_l_in, out_ref, flag_ref,
     sums, names, cos_ref, sin_ref, cos_far, sin_far, leaf_h, leaf_l, mats_h, mats_l, sems,
 ):
     pairs = (
@@ -405,14 +410,17 @@
     copies = [pltpu.make_async_copy(a, b, sems.at[n]) for n, (a, b) in enumerate(pairs)]
     for copy in copies:
         copy.start()
-    labels = x_ref[pl.ds(KEPT, LANES, stride=SLOTS), :]
+    labels = x_ref[pl.ds(LABEL_ROW, LANES, stride=SLOTS), :]
     names[...] = labels.T - 1.0
     flag_ref[0] = jnp.max(names[FLAG_LANE : FLAG_LANE + 1, :] + 1.0).astype(jnp.int32)
     column = iota((LANES, LANES), 1)
     filled = jnp.logical_and(labels > 0.0, column < KEPT)
     most = jnp.max(jnp.where(filled, column + 1, 0).astype(jnp.float32)).astype(jnp.int32)
     sums[...] = add_rows(x_ref, names, 0, SURE)
-    angle_rows(labels, dev_ref[0], cos_ref, sin_ref)
+    angles = x_ref[pl.ds(ANGLE_ROW, LANES, stride=SLOTS), :]
+    third = third_angles(x_ref, dev_ref[0])
+    peers = (peer0, peer1, peer2, peer3)
+    moved_rotations(angles, third, peers, dev_ref[0], cos_ref, sin_ref)
     for first in range(SURE, SLOTS, STEP):
 
         @pl.when(most > first)
@@ -421,8 +429,8 @@
 
     for copy in copies:
         copy.wait()
-    cos_ref[16:, :] = cos_far[16:, :]
-    sin_ref[16:, :] = sin_far[16:, :]
+    cos_ref[48:, :] = cos_far[48:, :]
+    sin_ref[48:, :] = sin_far[48:, :]
     state = []
     for c in range(8):
         block = sums[c * LANES : (c + 1) * LANES, :]
@@ -442,7 +450,7 @@
         out_ref[c * LANES : (c + 1) * LANES, :] = state[c].T
 
 
-def finish(arrived, prepared, box_count):
+def finish(arrived, peers, prepared, box_count):
     width = arrived.shape[1]
     table = pltpu.VMEM(prepared[0].shape, jnp.float32)
     return pl.pallas_call(
@@ -451,7 +459,7 @@
             jax.ShapeDtypeStruct((box_count, width), jnp.float32),
             jax.ShapeDtypeStruct((1,), jnp.int32),
         ],
-        in_specs=in_smem() + in_vmem(1) + anywhere(6),
+        in_specs=in_smem() + in_vmem(5) + anywhere(6),
         out_specs=in_vmem(1) + in_smem(),
         scratch_shapes=[
             pltpu.VMEM((box_count, 2 * width), jnp.float32),
@@ -462,12 +470,13 @@
         + [pltpu.VMEM(array.shape, array.dtype) for array in prepared]
         + [pltpu.SemaphoreType.DMA((len(prepared),))],
         compiler_params=params(),
-    )(own_number(), arrived, *prepared)
-
-
-def collect_kernel(x_ref, before_ref, sums, label_ref, flag_ref, names):
-    labels = x_ref[pl.ds(KEPT, LANES, stride=SLOTS), :]
-    label_ref[...] = labels
+    )(own_number(), arrived, *peers, *prepared)
+
+
+def collect_kernel(dev_ref, x_ref, before_ref, sums, angle_ref, flag_ref, names):
+    labels = x_ref[pl.ds(LABEL_ROW, LANES, stride=SLOTS), :]
+    angle_ref[:LANES, :] = x_ref[pl.ds(ANGLE_ROW, LANES, stride=SLOTS), :]
+    angle_ref[LANES:, :] = third_angles(x_ref, dev_ref[0])
     names[...] = labels.T - 1.0
     flag_ref[0] = jnp.max(names[FLAG_LANE : FLAG_LANE + 1, :] + 1.0).astype(jnp.int32)
     names[FLAG_LANE : FLAG_LANE + 1, :] = jnp.full((1, LANES), -1.0)
@@ -485,24 +494,26 @@
         collect_kernel,
         out_shape=[
             jax.ShapeDtypeStruct(sums.shape, jnp.float32),
-            jax.ShapeDtypeStruct((LANES, LANES), jnp.float32),
+            jax.ShapeDtypeStruct((LANES + 8, LANES), jnp.float32),
             jax.ShapeDtypeStruct((1,), jnp.int32),
         ],
-        in_specs=in_vmem(2),
+        in_specs=in_smem() + in_vmem(2),
         out_specs=in_vmem(2) + in_smem(),
         scratch_shapes=[pltpu.VMEM((LANES, LANES), jnp.float32)],
         compiler_params=params(),
-    )(arrived, sums)
+    )(own_number(), arrived, sums)
 
 
 def levels_kernel(
-    dev_ref, sums, labels_ref, cos_in, sin_in, leaf_h, leaf_l, mats_h, mats_l,
+    dev_ref, sums, angles_ref, peer0, peer1, peer2, peer3, cos_in, sin_in, leaf_h, leaf_l, mats_h, mats_l,
     out_ref, state, cos_ref, sin_ref,
 ):
     half = LANES // 2
     cos_ref[...] = cos_in[...]
     sin_ref[...] = sin_in[...]
-    angle_rows(labels_ref[...], dev_ref[0], cos_ref, sin_ref)
+    angles, third = angles_ref[:LANES, :], angles_ref[LANES:, :]
+    peers = (peer0, peer1, peer2, peer3)
+    moved_rotations(angles, third, peers, dev_ref[0], cos_ref, sin_ref)
 
     def leaf(c, carry):
         block = sums[pl.ds(pl.multiple_of(c * LANES, LANES), LANES), :]
@@ -551,53 +562,48 @@
     lax.fori_loop(0, 8, write, 0)
 
 
-def transform(sums, labels, prepared):
+def transform(sums, angles, peers, prepared):
     box_count, width = sums.shape[0], sums.shape[1] // 2
     table = pltpu.VMEM(prepared[0].shape, jnp.float32)
     return pl.pallas_call(
         levels_kernel,
         out_shape=jax.ShapeDtypeStruct((box_count, width), jnp.float32),
-        in_specs=in_smem() + in_vmem(8),
+        in_specs=in_smem() + in_vmem(12),
         out_specs=in_vmem(1)[0],
         scratch_shapes=[pltpu.VMEM((8, width, LANES), jnp.float32), table, table],
         compiler_params=params(),
-    )(own_number(), sums, labels, *prepared)
-
-
-def in_rounds(sources, owner, box, twiddle, prepared):
+    )(own_number(), sums, angles, *peers, *prepared)
+
+
+def in_rounds(sources, owner, box, peers, prepared):
+    twiddle = peers[0]
     box_count, width = twiddle.shape[1], sources.shape[1]
 
     def body(carry):
         number, sums, _, _ = carry
-        slots, labels = rank(number, owner, box, twiddle)
-        arrived = deliver(move(slots, labels, sources, labels))
+        arrived = deliver(pack(number, sources, owner, box, twiddle))
         return (number + 1, *collect(arrived, sums))
 
     start = (
         jnp.int32(0),
         jnp.zeros((box_count, 2 * width), jnp.float32),
-        jnp.zeros((LANES, LANES), jnp.float32),
+        jnp.zeros((LANES + 8, LANES), jnp.float32),
         jnp.ones((1,), jnp.int32),
     )
-    _, sums, labels, _ = lax.while_loop(lambda carry: carry[3][0] > 0, body, start)
-    return transform(sums, labels, prepared)
+    _, sums, angles, _ = lax.while_loop(lambda carry: carry[3][0] > 0, body, start)
+    return transform(sums, angles, peers, prepared)
 
 
 def local(sources, owner, box, leaf_op, level_ops, twiddle):
     box_count = twiddle.shape[1]
-    near = [swapped(twiddle, "gx", i) for i in (1, 2, 3)]
-    slots, labels = rank(jnp.int32(0), owner, box, twiddle)
-    slots, labels, *near = lax.optimization_barrier((slots, labels, *near))
-    near = jnp.concatenate([twiddle[2:6], near[0][2:3], near[1][2:4], near[2][2:3]], axis=0)
-    packed = move(slots, labels, sources, near)
-    far = [near] + [swapped(near, "gx", i) for i in (4, 8, 12)]
-    packed, *far = lax.optimization_barrier((packed, *far))
+    packed = pack(jnp.int32(0), sources, owner, box, twiddle)
     arrived = deliver(packed)
-    prepared = prepare(twiddle, far, leaf_op, level_ops)
-    blocks, flag = finish(arrived, prepared, box_count)
+    peers = [twiddle] + [swapped(twiddle, "gx", 4 * i) for i in range(1, 4)]
+    prepared = prepare(twiddle, leaf_op, level_ops)
+    blocks, flag = finish(arrived, peers, prepared, box_count)
     return lax.cond(
         flag[0] > 0,
-        lambda: in_rounds(sources, owner, box, twiddle, prepared),
+        lambda: in_rounds(sources, owner, box, peers, prepared),
         lambda: blocks,
     )
 

time: 71.9 us -> 66 us (0.918)
  waiting for transfers between devices: 27.9 us -> 24.3 us
  Pallas kernels: 22.9 us -> 20.6 us
  local copies, waits for them, and re-layouts: 2.3 us -> 4.44 us
  starting transfers between devices: 17.5 us -> 15.4 us
    all_to_all x1, waiting for transfers between devices: 27.9 us -> 2.66 us  [deliver(): lax.all_to_all(packed.reshape(-1, SLOTS, width), ('gx', 'gy'), split_axis...]
    ppermute x6 -> x3, waiting for transfers between devices: 0.02 us -> 21.6 us  [swapped(): lax.ppermute(shard, axis, [(i, i ^ shift) for i in range(lax.axis_size(ax...]
    pallas_call x2 -> x1, Pallas kernels: 7.62 us -> 4.47 us  [pack(): pl.pallas_call(pack_kernel, out_shape=jax.ShapeDtypeStruct((LANES * SLOTS...]
    unnamed x10 -> x20, local copies, waits for them, and re-layouts: 1.51 us -> 4.44 us
    ppermute x6 -> x3, starting transfers between devices: 6.79 us -> 3.95 us  [swapped(): lax.ppermute(shard, axis, [(i, i ^ shift) for i in range(lax.axis_size(ax...]
    pallas_call x1, Pallas kernels: 8.82 us -> 10.8 us  [finish(): pl.pallas_call(finish_kernel, out_shape=[jax.ShapeDtypeStruct((box_count,...]
    pallas_call x1, Pallas kernels: 6.42 us -> 5.37 us  [prepare(): pl.pallas_call(prepare_kernel, out_shape=[jax.ShapeDtypeStruct((levels *...]
    slice x4 -> x0, local copies, waits for them, and re-layouts: 0.78 us -> none  [the longest x1 0.76 us: local(): twiddle[2:6]]
  transfers between devices with their start and end apart: 7 -> 4, of which waited for: 1 -> 3; matrix products, arithmetic and copies ran while one was open for 1% -> 0% of each run, Pallas kernels for 20% -> 8%
where the time goes in v3:
time: 66 us; the launch traced here: 65.6 us
  waiting for transfers between devices  24.3 us (37%)
  Pallas kernels  20.6 us (31%)
  starting transfers between devices  15.4 us (23%)
  local copies, waits for them, and re-layouts  4.44 us (7%)
  between operations  0.7 us (1%)
    ppermute x3, waiting for transfers between devices, swapped(): lax.ppermute(shard, axis, [(i, i ^ shift) for i in range(lax.axis_size(ax...  21.6 us
    all_to_all x1, starting transfers between devices, deliver(): lax.all_to_all(packed.reshape(-1, SLOTS, width), ('gx', 'gy'), split_axis...  11.5 us
    pallas_call x1, Pallas kernels, finish(): pl.pallas_call(finish_kernel, out_shape=[jax.ShapeDtypeStruct((box_count,...  10.8 us
    pallas_call x1, Pallas kernels, prepare(): pl.pallas_call(prepare_kernel, out_shape=[jax.ShapeDtypeStruct((levels *...  5.37 us
    pallas_call x1, Pallas kernels, pack(): pl.pallas_call(pack_kernel, out_shape=jax.ShapeDtypeStruct((LANES * SLOTS...  4.47 us
    unnamed x20, local copies, waits for them, and re-layouts  4.44 us
    ppermute x3, starting transfers between devices, swapped(): lax.ppermute(shard, axis, [(i, i ^ shift) for i in range(lax.axis_size(ax...  3.95 us
    all_to_all x1, waiting for transfers between devices, deliver(): lax.all_to_all(packed.reshape(-1, SLOTS, width), ('gx', 'gy'), split_axis...  2.66 us
  transfers between devices with their start and end apart: 4, of which 3 were waited for; matrix products, arithmetic and copies ran while one was open for 0% of the time, Pallas kernels for 8%

profile of v3, /device:TPU:1, one launch (start us, length us, event | category | flops | bytes accessed | tf_op | source)
XLA Modules:
  0.0 65.6 jit_solution(10783983558569969526)
XLA Ops:
  0.0 4.5 %shard_map.66 = f32[5120,128]{1,0:T(8,128)S(1)} custom-call(s32[1]{0:T(128)} %constant.48.clone.1.round_ref, s32[1]{0:T(128)} %bitcast.8.dev_ref, s32[16,128]{1,0:T(8,128)} %bitcast.31, s32[16,128]{1,0:T(8,128)} %bitcast.33, f32[7,1024]{1,0:T(8,128)} %peer0.1, f32[2048,128]{1,0:T(8,128)} %src_hbm.1), custom_call_target="tpu_custom_call" | custom-call | tf_op jit(solution)/shard_map/pallas_call | solution.py:178
  4.5 0.0 copy-start.2
  4.5 1.5 %copy-done.2 = f32[5120,128]{1,0:T(8,128)} copy-done((f32[5120,128]{1,0:T(8,128)}, f32[5120,128]{1,0:T(8,128)S(1)}, u32[]{:S(2)}) %copy-start.2) | copy-done | bytes 2621464
  6.0 0.0 copy-start.4
  6.0 11.5 %all-to-all-start.1 = ((f32[128,40,128]{2,1,0:T(8,128)}), f32[128,40,128]{2,1,0:T(8,128)S(1)}, u32[]{:S(2)}, u32[]{:S(2)}) async-start(f32[128,40,128]{2,1,0:T(8,128)} %bitcast.30), calls=%async_computation.1 | async-start | bytes 5242880 | tf_op jit(solution)/shard_map/all_to_all | solution.py:205
  17.5 1.5 %collective-permute-start = (f32[7,1024]{1,0:T(8,128)}, f32[7,1024]{1,0:T(8,128)S(1)}, u32[]{:S(2)}, u32[]{:S(2)}) collective-permute-start(f32[7,1024]{1,0:T(8,128)} %peer0.1), channel_id=1, source_target_pairs={{0,32},{8,40},{16,48},{24,56},{32,0},{40,8},{48,16},{56,24},{64,96... | collective-permute-start | bytes 86024 | tf_op jit(solution)/shard_map/ppermute | solution.py:13
  19.0 2.4 %collective-permute-start.1 = (f32[7,1024]{1,0:T(8,128)}, f32[7,1024]{1,0:T(8,128)S(1)}, u32[]{:S(2)}, u32[]{:S(2)}) collective-permute-start(f32[7,1024]{1,0:T(8,128)} %peer0.1), channel_id=1, source_target_pairs={{0,64},{8,72},{16,80},{24,88},{32,96},{40,104},{48,112},{56,120},{... | collective-permute-start | bytes 86024 | tf_op jit(solution)/shard_map/ppermute | solution.py:13
  21.4 0.1 collective-permute-start.2
  21.4 0.0 copy-done.4
  21.5 0.0 copy-start.3
  21.5 1.5 %copy-done.3 = f32[7,2,2,2,64,64]{5,4,3,2,1,0:T(8,128)S(1)} copy-done((f32[7,2,2,2,64,64]{5,4,3,2,1,0:T(8,128)S(1)}, f32[7,2,2,2,64,64]{5,4,3,2,1,0:T(8,128)}, u32[]{:S(2)}) %copy-start.3) | copy-done | bytes 917528
  23.0 5.4 %shard_map.67 = (f32[56,128]{1,0:T(8,128)}, f32[56,128]{1,0:T(8,128)}, bf16[128,128]{1,0:T(8,128)(2,1)}, bf16[128,128]{1,0:T(8,128)(2,1)}, bf16[7,256,256]{2,1,0:T(8,128)(2,1)}, /*index=5*/bf16[7,256,256]{2,1,0:T(8,128)(2,1)}) custom-call(s32[1]{0:T(128)} %bitcast.8.dev_ref, f32[7,1024]{1,0:T(8,128)} %peer0.1, f32[2,64,64]{2,1,0:T(8,128)S(1)} %copy-done.4, ...), custom_call_target="tpu_custom_call" | custom-call | tf_op jit(solution)/shard_map/pallas_call | solution.py:291
  28.3 0.0 copy-start.5
  28.3 0.0 copy-start.6
  28.3 0.0 copy-start.7
  28.3 19.4 %collective-permute-done.peer1 = f32[7,1024]{1,0:T(8,128)S(1)} collective-permute-done((f32[7,1024]{1,0:T(8,128)}, f32[7,1024]{1,0:T(8,128)S(1)}, u32[]{:S(2)}, u32[]{:S(2)}) %collective-permute-start) | collective-permute-done | bytes 28704 | tf_op jit(solution)/shard_map/ppermute | solution.py:13
  47.8 0.0 copy-start.8
  47.8 2.2 %collective-permute-done.1.peer2 = f32[7,1024]{1,0:T(8,128)S(1)} collective-permute-done((f32[7,1024]{1,0:T(8,128)}, f32[7,1024]{1,0:T(8,128)S(1)}, u32[]{:S(2)}, u32[]{:S(2)}) %collective-permute-start.1) | collective-permute-done | bytes 28704 | tf_op jit(solution)/shard_map/ppermute | solution.py:13
  50.0 0.0 copy-start.9
  50.0 0.0 collective-permute-done.2.peer3
  50.0 0.0 copy-start.10
  50.0 0.0 copy-done.8
  50.0 0.6 copy-done.9
  50.6 0.0 copy-done.10
  50.6 2.7 %all-to-all-done.1 = f32[128,40,128]{2,1,0:T(8,128)S(1)} async-done(((f32[128,40,128]{2,1,0:T(8,128)}), f32[128,40,128]{2,1,0:T(8,128)S(1)}, u32[]{:S(2)}, u32[]{:S(2)}) %all-to-all-start.1) | async-done | bytes 2621472 | tf_op jit(solution)/shard_map/all_to_all | solution.py:205
  53.3 10.8 %shard_map.68 = (f32[1024,128]{1,0:T(8,128)S(1)}, s32[1]{0:T(128)}) custom-call(s32[1]{0:T(128)} %bitcast.8.dev_ref, f32[5120,128]{1,0:T(8,128)S(1)} %bitcast.29, f32[7,1024]{1,0:T(8,128)} %peer0.1, f32[7,1024]{1,0:T(8,128)} %copy-done.8, f32[7,1024]{1,0:T(8,128)} %copy-done.9, f32[7,1024]{1,0:T(8,128)} %copy-done.10, f32[56,128]{1,0:T(8,128)} %get-tuple-element.100.cos_in, ...), custom_call_target="tpu_custom_call" | custom-call | tf_op jit(solution)/shard_map/pallas_call | solution.py:456
  64.7 0.0 copy-done.5
  64.7 0.0 copy-done.6
  64.7 0.0 copy-done.7
  64.8 0.0 copy-start.11
  64.8 0.8 %copy-done.11 = f32[1024,128]{1,0:T(8,128)} copy-done((f32[1024,128]{1,0:T(8,128)}, f32[1024,128]{1,0:T(8,128)S(1)}, u32[]{:S(2)}) %copy-start.11) | copy-done | bytes 524312
  (1 shorter events, 0.0 us)
Async XLA Ops:
  4.5 1.5 %copy-start.2 = (f32[5120,128]{1,0:T(8,128)}, f32[5120,128]{1,0:T(8,128)S(1)}, u32[]{:S(2)}) copy-start(f32[5120,128]{1,0:T(8,128)S(1)} %shard_map.66) | copy-start | bytes 7864324
  6.0 15.5 %copy-start.4 = (f32[2,64,64]{2,1,0:T(8,128)S(1)}, f32[2,64,64]{2,1,0:T(8,128)}, u32[]{:S(2)}) copy-start(f32[2,64,64]{2,1,0:T(8,128)} %leaf_ref.1) | copy-start | bytes 98308
  6.0 47.3 %all-to-all-start.1 = ((f32[128,40,128]{2,1,0:T(8,128)}), f32[128,40,128]{2,1,0:T(8,128)S(1)}, u32[]{:S(2)}, u32[]{:S(2)}) async-start(f32[128,40,128]{2,1,0:T(8,128)} %bitcast.30), calls=%async_computation.1 | async-start | bytes 5242880 | tf_op jit(solution)/shard_map/all_to_all | solution.py:205
  17.5 30.3 %collective-permute-start = (f32[7,1024]{1,0:T(8,128)}, f32[7,1024]{1,0:T(8,128)S(1)}, u32[]{:S(2)}, u32[]{:S(2)}) collective-permute-start(f32[7,1024]{1,0:T(8,128)} %peer0.1), channel_id=1, source_target_pairs={{0,32},{8,40},{16,48},{24,56},{32,0},{40,8},{48,16},{56,24},{64,96... | collective-permute-start | bytes 86024 | tf_op jit(solution)/shard_map/ppermute | solution.py:13
  19.0 31.0 %collective-permute-start.1 = (f32[7,1024]{1,0:T(8,128)}, f32[7,1024]{1,0:T(8,128)S(1)}, u32[]{:S(2)}, u32[]{:S(2)}) collective-permute-start(f32[7,1024]{1,0:T(8,128)} %peer0.1), channel_id=1, source_target_pairs={{0,64},{8,72},{16,80},{24,88},{32,96},{40,104},{48,112},{56,120},{... | collective-permute-start | bytes 86024 | tf_op jit(solution)/shard_map/ppermute | solution.py:13
  21.4 28.6 %collective-permute-start.2 = (f32[7,1024]{1,0:T(8,128)}, f32[7,1024]{1,0:T(8,128)S(1)}, u32[]{:S(2)}, u32[]{:S(2)}) collective-permute-start(f32[7,1024]{1,0:T(8,128)} %peer0.1), channel_id=1, source_target_pairs={{0,96},{8,104},{16,112},{24,120},{32,64},{40,72},{48,80},{56,88},{... | collective-permute-start | bytes 86024 | tf_op jit(solution)/shard_map/ppermute | solution.py:13
  21.5 1.5 %copy-start.3 = (f32[7,2,2,2,64,64]{5,4,3,2,1,0:T(8,128)S(1)}, f32[7,2,2,2,64,64]{5,4,3,2,1,0:T(8,128)}, u32[]{:S(2)}) copy-start(f32[7,2,2,2,64,64]{5,4,3,2,1,0:T(8,128)} %ops_ref.1) | copy-start | bytes 2752516
  28.3 36.4 %copy-start.5 = (bf16[7,256,256]{2,1,0:T(8,128)(2,1)S(1)}, bf16[7,256,256]{2,1,0:T(8,128)(2,1)}, u32[]{:S(2)}) copy-start(bf16[7,256,256]{2,1,0:T(8,128)(2,1)} %get-tuple-element.104.mats_h_in) | copy-start | bytes 2752516
  28.3 36.4 %copy-start.6 = (s32[2048,1]{0,1:T(1,128)S(1)}, s32[2048,1]{0,1:T(1,128)}, u32[]{:S(2)}) copy-start(s32[2048,1]{0,1:T(1,128)} %param.11) | copy-start | bytes 24580
  28.3 36.4 %copy-start.7 = (s32[2048]{0:T(1024)S(1)}, s32[2048]{0:T(1024)}, u32[]{:S(2)}) copy-start(s32[2048]{0:T(1024)} %param.12) | copy-start | bytes 24580
  47.8 2.2 %copy-start.8 = (f32[7,1024]{1,0:T(8,128)}, f32[7,1024]{1,0:T(8,128)S(1)}, u32[]{:S(2)}) copy-start(f32[7,1024]{1,0:T(8,128)S(1)} %collective-permute-done.peer1) | copy-start | bytes 86020
  50.0 0.6 copy-start.9
  50.0 0.6 copy-start.10
  64.8 0.8 %copy-start.11 = (f32[1024,128]{1,0:T(8,128)}, f32[1024,128]{1,0:T(8,128)S(1)}, u32[]{:S(2)}) copy-start(f32[1024,128]{1,0:T(8,128)S(1)} %get-tuple-element.226) | copy-start | bytes 1572868

commit v4 on v3

--- a/solution.py
+++ b/solution.py
@@ -239,14 +239,18 @@
     return owner, index
 
 
-def rotations(held, row, column, level, cos_ref, sin_ref):
-    pick = jnp.where(row == iota((held.shape[0], 8 * LANES), 0), 1.0, 0.0)
-    spread = exact_dot(held, pick, (0, 0))
+def picked(held, row, column):
+    pick = jnp.where(row == iota((held.shape[0], 8 * LANES), 0), 1.0, 0.0).astype(jnp.bfloat16)
+    high = held.astype(jnp.bfloat16)
+    rest = held - high.astype(jnp.float32)
+    parts = (high, *split(rest))
+    spread = sum(
+        lax.dot_general(part, pick, (((0,), (0,)), ((), ())), preferred_element_type=jnp.float32)
+        for part in parts
+    )
     mine = column == iota((LANES, 8 * LANES), 0)
     angle = jnp.sum(jnp.where(mine, spread, 0.0), axis=0, keepdims=True)
-    angle = jnp.concatenate([angle[:, c * LANES : (c + 1) * LANES] for c in range(8)], axis=0)
-    cos_ref[level * 8 : level * 8 + 8, :] = jnp.cos(angle)
-    sin_ref[level * 8 : level * 8 + 8, :] = jnp.sin(angle)
+    return jnp.concatenate([angle[:, c * LANES : (c + 1) * LANES] for c in range(8)], axis=0)
 
 
 def split(value):
@@ -263,7 +267,9 @@
     _, index = twiddle_place(6, iota((1, 8 * LANES), 1), dev_ref[0])
     angles = [twiddle_ref[6:7, c * LANES : (c + 1) * LANES] for c in range(8)]
     row, column = jnp.right_shift(index, 7), jnp.bitwise_and(index, LANES - 1)
-    rotations(jnp.concatenate(angles, axis=0), row, column, 6, cos_ref, sin_ref)
+    angle = picked(jnp.concatenate(angles, axis=0), row, column)
+    cos_ref[48:56, :] = jnp.cos(angle)
+    sin_ref[48:56, :] = jnp.sin(angle)
 
     def block(real, imag):
         top = jnp.concatenate([real, imag], axis=1)
@@ -319,6 +325,7 @@
 
 def moved_rotations(angles, third, peers, device, cos_ref, sin_ref):
     position = iota((1, 8 * LANES), 1)
+    angle = []
     for level in range(6):
         owner, index = twiddle_place(level, position, device)
         if level < 3:
@@ -340,7 +347,10 @@
             row = jnp.right_shift(jnp.bitwise_xor(owner, device), 5)
             row = row + 4 * jnp.bitwise_and(jnp.right_shift(index, 7), taken - 1)
             column = jnp.bitwise_and(index, LANES - 1)
-        rotations(held, row, column, level, cos_ref, sin_ref)
+        angle.append(picked(held, row, column))
+    angle = jnp.concatenate(angle, axis=0)
+    cos_ref[0:48, :] = jnp.cos(angle)
+    sin_ref[0:48, :] = jnp.sin(angle)
 
 
 def third_angles(x_ref, device):
@@ -400,8 +410,9 @@
 
 def finish_kernel(
     dev_ref, x_ref, peer0, peer1, peer2, peer3,
-    cos_in, sin_in, leaf_h_in, leaf_l_in, mats_h_in, mats_l_in, out_ref, flag_ref,
-    sums, names, cos_ref, sin_ref, cos_far, sin_far, leaf_h, leaf_l, mats_h, mats_l, sems,
+    cos_in, sin_in, leaf_h_in, leaf_l_in, mats_h_in, mats_l_in,
+    out_ref, flag_ref, cos_ref, sin_ref,
+    sums, names, cos_far, sin_far, leaf_h, leaf_l, mats_h, mats_l, sems,
 ):
     pairs = (
         (cos_in, cos_far), (sin_in, sin_far), (leaf_h_in, leaf_h), (leaf_l_in, leaf_l),
@@ -452,20 +463,20 @@
 
 def finish(arrived, peers, prepared, box_count):
     width = arrived.shape[1]
-    table = pltpu.VMEM(prepared[0].shape, jnp.float32)
+    table = jax.ShapeDtypeStruct(prepared[0].shape, jnp.float32)
     return pl.pallas_call(
         finish_kernel,
         out_shape=[
             jax.ShapeDtypeStruct((box_count, width), jnp.float32),
             jax.ShapeDtypeStruct((1,), jnp.int32),
+            table,
+            table,
         ],
         in_specs=in_smem() + in_vmem(5) + anywhere(6),
-        out_specs=in_vmem(1) + in_smem(),
+        out_specs=in_vmem(1) + in_smem() + in_vmem(2),
         scratch_shapes=[
             pltpu.VMEM((box_count, 2 * width), jnp.float32),
             pltpu.VMEM((LANES, LANES), jnp.float32),
-            table,
-            table,
         ]
         + [pltpu.VMEM(array.shape, array.dtype) for array in prepared]
         + [pltpu.SemaphoreType.DMA((len(prepared),))],
@@ -473,10 +484,8 @@
     )(own_number(), arrived, *peers, *prepared)
 
 
-def collect_kernel(dev_ref, x_ref, before_ref, sums, angle_ref, flag_ref, names):
+def collect_kernel(x_ref, before_ref, sums, flag_ref, names):
     labels = x_ref[pl.ds(LABEL_ROW, LANES, stride=SLOTS), :]
-    angle_ref[:LANES, :] = x_ref[pl.ds(ANGLE_ROW, LANES, stride=SLOTS), :]
-    angle_ref[LANES:, :] = third_angles(x_ref, dev_ref[0])
     names[...] = labels.T - 1.0
     flag_ref[0] = jnp.max(names[FLAG_LANE : FLAG_LANE + 1, :] + 1.0).astype(jnp.int32)
     names[FLAG_LANE : FLAG_LANE + 1, :] = jnp.full((1, LANES), -1.0)
@@ -494,26 +503,17 @@
         collect_kernel,
         out_shape=[
             jax.ShapeDtypeStruct(sums.shape, jnp.float32),
-            jax.ShapeDtypeStruct((LANES + 8, LANES), jnp.float32),
             jax.ShapeDtypeStruct((1,), jnp.int32),
         ],
-        in_specs=in_smem() + in_vmem(2),
-        out_specs=in_vmem(2) + in_smem(),
+        in_specs=in_vmem(2),
+        out_specs=in_vmem(1) + in_smem(),
         scratch_shapes=[pltpu.VMEM((LANES, LANES), jnp.float32)],
         compiler_params=params(),
-    )(own_number(), arrived, sums)
-
-
-def levels_kernel(
-    dev_ref, sums, angles_ref, peer0, peer1, peer2, peer3, cos_in, sin_in, leaf_h, leaf_l, mats_h, mats_l,
-    out_ref, state, cos_ref, sin_ref,
-):
+    )(arrived, sums)
+
+
+def levels_kernel(sums, cos_ref, sin_ref, leaf_h, leaf_l, mats_h, mats_l, out_ref, state):
     half = LANES // 2
-    cos_ref[...] = cos_in[...]
-    sin_ref[...] = sin_in[...]
-    angles, third = angles_ref[:LANES, :], angles_ref[LANES:, :]
-    peers = (peer0, peer1, peer2, peer3)
-    moved_rotations(angles, third, peers, dev_ref[0], cos_ref, sin_ref)
 
     def leaf(c, carry):
         block = sums[pl.ds(pl.multiple_of(c * LANES, LANES), LANES), :]
@@ -562,36 +562,33 @@
     lax.fori_loop(0, 8, write, 0)
 
 
-def transform(sums, angles, peers, prepared):
+def transform(sums, prepared):
     box_count, width = sums.shape[0], sums.shape[1] // 2
-    table = pltpu.VMEM(prepared[0].shape, jnp.float32)
     return pl.pallas_call(
         levels_kernel,
         out_shape=jax.ShapeDtypeStruct((box_count, width), jnp.float32),
-        in_specs=in_smem() + in_vmem(12),
+        in_specs=in_vmem(7),
         out_specs=in_vmem(1)[0],
-        scratch_shapes=[pltpu.VMEM((8, width, LANES), jnp.float32), table, table],
+        scratch_shapes=[pltpu.VMEM((8, width, LANES), jnp.float32)],
         compiler_params=params(),
-    )(own_number(), sums, angles, *peers, *prepared)
-
-
-def in_rounds(sources, owner, box, peers, prepared):
-    twiddle = peers[0]
+    )(sums, *prepared)
+
+
+def in_rounds(sources, owner, box, twiddle, prepared):
     box_count, width = twiddle.shape[1], sources.shape[1]
 
     def body(carry):
-        number, sums, _, _ = carry
+        number, sums, _ = carry
         arrived = deliver(pack(number, sources, owner, box, twiddle))
         return (number + 1, *collect(arrived, sums))
 
     start = (
         jnp.int32(0),
         jnp.zeros((box_count, 2 * width), jnp.float32),
-        jnp.zeros((LANES + 8, LANES), jnp.float32),
         jnp.ones((1,), jnp.int32),
     )
-    _, sums, angles, _ = lax.while_loop(lambda carry: carry[3][0] > 0, body, start)
-    return transform(sums, angles, peers, prepared)
+    _, sums, _ = lax.while_loop(lambda carry: carry[2][0] > 0, body, start)
+    return transform(sums, prepared)
 
 
 def local(sources, owner, box, leaf_op, level_ops, twiddle):
@@ -600,10 +597,10 @@
     arrived = deliver(packed)
     peers = [twiddle] + [swapped(twiddle, "gx", 4 * i) for i in range(1, 4)]
     prepared = prepare(twiddle, leaf_op, level_ops)
-    blocks, flag = finish(arrived, peers, prepared, box_count)
+    blocks, flag, *tables = finish(arrived, peers, prepared, box_count)
     return lax.cond(
         flag[0] > 0,
-        lambda: in_rounds(sources, owner, box, peers, prepared),
+        lambda: in_rounds(sources, owner, box, twiddle, [*tables, *prepared[2:]]),
         lambda: blocks,
     )
 

time: 66 us -> 63.7 us (0.965)
  Pallas kernels: 20.6 us -> 18 us
  waiting for transfers between devices: 24.3 us -> 26.5 us
  local copies, waits for them, and re-layouts: 4.44 us -> 3.01 us
    pallas_call x1, Pallas kernels: 10.8 us -> 9.09 us  [finish(): pl.pallas_call(finish_kernel, out_shape=[jax.ShapeDtypeStruct((box_count,...]
    unnamed x20 -> x12, local copies, waits for them, and re-layouts: 4.44 us -> 3.01 us
    all_to_all x1, waiting for transfers between devices: 2.66 us -> 3.93 us  [deliver(): lax.all_to_all(packed.reshape(-1, SLOTS, width), ('gx', 'gy'), split_axis...]
    pallas_call x1, Pallas kernels: 5.37 us -> 4.47 us  [prepare(): pl.pallas_call(prepare_kernel, out_shape=[jax.ShapeDtypeStruct((levels *...]
    ppermute x3, waiting for transfers between devices: 21.6 us -> 22.5 us  [swapped(): lax.ppermute(shard, axis, [(i, i ^ shift) for i in range(lax.axis_size(ax...]
  transfers between devices with their start and end apart: 4 -> 4, of which waited for: 3 -> 2; matrix products, arithmetic and copies ran while one was open for 0% -> 0% of each run, Pallas kernels for 8% -> 7%
where the time goes in v4:
time: 63.7 us; the launch traced here: 63.4 us
  waiting for transfers between devices  26.5 us (42%)
  Pallas kernels  18 us (28%)
  starting transfers between devices  14.8 us (23%)
  local copies, waits for them, and re-layouts  3.01 us (5%)
  between operations  0.86 us (1%)
    ppermute x3, waiting for transfers between devices, swapped(): lax.ppermute(shard, axis, [(i, i ^ shift) for i in range(lax.axis_size(ax...  22.5 us
    all_to_all x1, starting transfers between devices, deliver(): lax.all_to_all(packed.reshape(-1, SLOTS, width), ('gx', 'gy'), split_axis...  11.5 us
    pallas_call x1, Pallas kernels, finish(): pl.pallas_call(finish_kernel, out_shape=[jax.ShapeDtypeStruct((box_count,...  9.09 us
    pallas_call x1, Pallas kernels, pack(): pl.pallas_call(pack_kernel, out_shape=jax.ShapeDtypeStruct((LANES * SLOTS...  4.47 us
    pallas_call x1, Pallas kernels, prepare(): pl.pallas_call(prepare_kernel, out_shape=[jax.ShapeDtypeStruct((levels *...  4.47 us
    all_to_all x1, waiting for transfers between devices, deliver(): lax.all_to_all(packed.reshape(-1, SLOTS, width), ('gx', 'gy'), split_axis...  3.93 us
    ppermute x3, starting transfers between devices, swapped(): lax.ppermute(shard, axis, [(i, i ^ shift) for i in range(lax.axis_size(ax...  3.35 us
    unnamed x12, local copies, waits for them, and re-layouts  3.01 us
  transfers between devices with their start and end apart: 4, of which 2 were waited for; matrix products, arithmetic and copies ran while one was open for 0% of the time, Pallas kernels for 7%

profile of v4, /device:TPU:1, one launch (start us, length us, event | category | flops | bytes accessed | tf_op | source)
XLA Modules:
  0.0 63.4 jit_solution(9182443811793471508)
XLA Ops:
  0.0 4.5 %shard_map.66 = f32[5120,128]{1,0:T(8,128)S(1)} custom-call(s32[1]{0:T(128)} %constant.36.clone.1.round_ref, s32[1]{0:T(128)} %bitcast.7.dev_ref, s32[16,128]{1,0:T(8,128)} %bitcast.30, s32[16,128]{1,0:T(8,128)} %bitcast.32, f32[7,1024]{1,0:T(8,128)} %peer0.1, f32[2048,128]{1,0:T(8,128)} %src_hbm.1), custom_call_target="tpu_custom_call" | custom-call | tf_op jit(solution)/shard_map/pallas_call | solution.py:178
  4.5 0.0 copy-start.2
  4.5 1.5 %copy-done.2 = f32[5120,128]{1,0:T(8,128)} copy-done((f32[5120,128]{1,0:T(8,128)}, f32[5120,128]{1,0:T(8,128)S(1)}, u32[]{:S(2)}) %copy-start.2) | copy-done | bytes 2621464
  6.0 0.0 copy-start.6
  6.0 0.0 copy-start.4
  6.0 11.5 %all-to-all-start.1 = ((f32[128,40,128]{2,1,0:T(8,128)}), f32[128,40,128]{2,1,0:T(8,128)S(1)}, u32[]{:S(2)}, u32[]{:S(2)}) async-start(f32[128,40,128]{2,1,0:T(8,128)} %bitcast.29), calls=%async_computation.1 | async-start | bytes 5242880 | tf_op jit(solution)/shard_map/all_to_all | solution.py:205
  17.5 0.0 copy-done.6
  17.5 2.7 %collective-permute-start.2 = (f32[7,1024]{1,0:T(8,128)S(1)}, f32[7,1024]{1,0:T(8,128)S(1)}, u32[]{:S(2)}, u32[]{:S(2)}) collective-permute-start(f32[7,1024]{1,0:T(8,128)S(1)} %copy-done.6), channel_id=1, source_target_pairs={{0,96},{8,104},{16,112},{24,120},{32,64},{40,72},{48,80},{56,88},{... | collective-permute-start | bytes 86024 | tf_op jit(solution)/shard_map/ppermute | solution.py:13
  20.2 0.6 collective-permute-start.1
  20.8 0.1 collective-permute-start
  20.9 0.0 copy-done.4
  20.9 0.0 copy-start.3
  20.9 1.5 %copy-done.3 = f32[7,2,2,2,64,64]{5,4,3,2,1,0:T(8,128)S(1)} copy-done((f32[7,2,2,2,64,64]{5,4,3,2,1,0:T(8,128)S(1)}, f32[7,2,2,2,64,64]{5,4,3,2,1,0:T(8,128)}, u32[]{:S(2)}) %copy-start.3) | copy-done | bytes 917528
  22.4 4.5 %shard_map.67 = (f32[56,128]{1,0:T(8,128)S(1)}, f32[56,128]{1,0:T(8,128)S(1)}, bf16[128,128]{1,0:T(8,128)(2,1)S(1)}, bf16[128,128]{1,0:T(8,128)(2,1)S(1)}, bf16[...) custom-call(s32[1]{0:T(128)} %bitcast.7.dev_ref, f32[7,1024]{1,0:T(8,128)S(1)} %copy-done.6, ...), custom_call_target="tpu_custom_call" | custom-call | tf_op jit(solution)/shard_map/pallas_call | solution.py:297
  26.8 0.0 copy-start.8
  26.8 0.0 copy-start.9
  26.8 22.5 %collective-permute-done.2.peer3 = f32[7,1024]{1,0:T(8,128)S(1)} collective-permute-done((f32[7,1024]{1,0:T(8,128)S(1)}, f32[7,1024]{1,0:T(8,128)S(1)}, u32[]{:S(2)}, u32[]{:S(2)}) %collective-permute-start.2) | collective-permute-done | bytes 28704 | tf_op jit(solution)/shard_map/ppermute | solution.py:13
  49.4 0.0 collective-permute-done.1.peer2
  49.4 0.0 collective-permute-done.peer1
  49.4 3.9 %all-to-all-done.1 = f32[128,40,128]{2,1,0:T(8,128)S(1)} async-done(((f32[128,40,128]{2,1,0:T(8,128)}), f32[128,40,128]{2,1,0:T(8,128)S(1)}, u32[]{:S(2)}, u32[]{:S(2)}) %all-to-all-start.1) | async-done | bytes 2621472 | tf_op jit(solution)/shard_map/all_to_all | solution.py:205
  53.3 9.1 %shard_map.68 = (f32[1024,128]{1,0:T(8,128)}, s32[1]{0:T(128)}, f32[56,128]{1,0:T(8,128)}, f32[56,128]{1,0:T(8,128)}) custom-call(s32[1]{0:T(128)} %bitcast.7.dev_ref, f32[5120,128]{1,0:T(8,128)S(1)} %bitcast.28, f32[7,1024]{1,0:T(8,128)S(1)} %copy-done.6, f32[7,1024]{1,0:T(8,128)S(1)} %collective-permute-done.peer1, ...), custom_call_target="tpu_custom_call" | custom-call | tf_op jit(solution)/shard_map/pallas_call | solution.py:467
  63.0 0.0 copy-done.8
  63.0 0.0 copy-done.9
  63.0 0.2 conditional.1
Async XLA Ops:
  4.5 1.5 %copy-start.2 = (f32[5120,128]{1,0:T(8,128)}, f32[5120,128]{1,0:T(8,128)S(1)}, u32[]{:S(2)}) copy-start(f32[5120,128]{1,0:T(8,128)S(1)} %shard_map.66) | copy-start | bytes 7864324
  6.0 11.5 %copy-start.6 = (f32[7,1024]{1,0:T(8,128)S(1)}, f32[7,1024]{1,0:T(8,128)}, u32[]{:S(2)}) copy-start(f32[7,1024]{1,0:T(8,128)} %peer0.1) | copy-start | bytes 86020
  6.0 14.9 %copy-start.4 = (f32[2,64,64]{2,1,0:T(8,128)S(1)}, f32[2,64,64]{2,1,0:T(8,128)}, u32[]{:S(2)}) copy-start(f32[2,64,64]{2,1,0:T(8,128)} %leaf_ref.1) | copy-start | bytes 98308
  6.0 47.3 %all-to-all-start.1 = ((f32[128,40,128]{2,1,0:T(8,128)}), f32[128,40,128]{2,1,0:T(8,128)S(1)}, u32[]{:S(2)}, u32[]{:S(2)}) async-start(f32[128,40,128]{2,1,0:T(8,128)} %bitcast.29), calls=%async_computation.1 | async-start | bytes 5242880 | tf_op jit(solution)/shard_map/all_to_all | solution.py:205
  17.5 31.8 %collective-permute-start.2 = (f32[7,1024]{1,0:T(8,128)S(1)}, f32[7,1024]{1,0:T(8,128)S(1)}, u32[]{:S(2)}, u32[]{:S(2)}) collective-permute-start(f32[7,1024]{1,0:T(8,128)S(1)} %copy-done.6), channel_id=1, source_target_pairs={{0,96},{8,104},{16,112},{24,120},{32,64},{40,72},{48,80},{56,88},{... | collective-permute-start | bytes 86024 | tf_op jit(solution)/shard_map/ppermute | solution.py:13
  20.2 29.2 %collective-permute-start.1 = (f32[7,1024]{1,0:T(8,128)S(1)}, f32[7,1024]{1,0:T(8,128)S(1)}, u32[]{:S(2)}, u32[]{:S(2)}) collective-permute-start(f32[7,1024]{1,0:T(8,128)S(1)} %copy-done.6), channel_id=1, source_target_pairs={{0,64},{8,72},{16,80},{24,88},{32,96},{40,104},{48,112},{56,120},{... | collective-permute-start | bytes 86024 | tf_op jit(solution)/shard_map/ppermute | solution.py:13
  20.8 28.6 %collective-permute-start = (f32[7,1024]{1,0:T(8,128)S(1)}, f32[7,1024]{1,0:T(8,128)S(1)}, u32[]{:S(2)}, u32[]{:S(2)}) collective-permute-start(f32[7,1024]{1,0:T(8,128)S(1)} %copy-done.6), channel_id=1, source_target_pairs={{0,32},{8,40},{16,48},{24,56},{32,0},{40,8},{48,16},{56,24},{64,96... | collective-permute-start | bytes 86024 | tf_op jit(solution)/shard_map/ppermute | solution.py:13
  20.9 1.5 %copy-start.3 = (f32[7,2,2,2,64,64]{5,4,3,2,1,0:T(8,128)S(1)}, f32[7,2,2,2,64,64]{5,4,3,2,1,0:T(8,128)}, u32[]{:S(2)}) copy-start(f32[7,2,2,2,64,64]{5,4,3,2,1,0:T(8,128)} %ops_ref.1) | copy-start | bytes 2752516
  26.8 36.2 %copy-start.8 = (s32[2048,1]{0,1:T(1,128)S(1)}, s32[2048,1]{0,1:T(1,128)}, u32[]{:S(2)}) copy-start(s32[2048,1]{0,1:T(1,128)} %param.11) | copy-start | bytes 24580
  26.8 36.2 %copy-start.9 = (s32[2048]{0:T(1024)S(1)}, s32[2048]{0:T(1024)}, u32[]{:S(2)}) copy-start(s32[2048]{0:T(1024)} %param.12) | copy-start | bytes 24580

commit v5 on v4

--- a/solution.py
+++ b/solution.py
@@ -20,7 +20,7 @@
 ANGLE_ROW = KEPT + 1
 ANGLE_LANES = (0, 32, 64)
 THIRD_ROW = KEPT - 1
-SURE = 16
+SURE = 24
 STEP = 4
 
 
@@ -40,14 +40,9 @@
     return lax.broadcasted_iota(jnp.int32, shape, axis)
 
 
-def exact_dot(left, right, contract=(1, 0)):
-    return lax.dot_general(
-        left,
-        right,
-        (((contract[0],), (contract[1],)), ((), ())),
-        precision=lax.Precision.HIGHEST,
-        preferred_element_type=jnp.float32,
-    )
+def thirds(value):
+    high = value.astype(jnp.bfloat16)
+    return (high, *split(value - high.astype(jnp.float32)))
 
 
 def angles_for_all(twiddle_ref, level, lane):
@@ -64,12 +59,13 @@
         rows = jnp.where(first == g, part, rows)
     rows = jnp.where(jnp.right_shift(cols, 4 + level) == group, rows, 0.0)
     fold = jnp.where(cols == lane + jnp.bitwise_and(dest, width - 1), 1.0, 0.0)
-    return exact_dot(rows, fold)
+    fold = fold.astype(jnp.bfloat16)
+    return sum(jnp.dot(part, fold, preferred_element_type=jnp.float32) for part in thirds(rows))
 
 
 def pack_kernel(
     round_ref, dev_ref, owner_hbm, box_hbm, twiddle_hbm, src_hbm, out_ref,
-    owner_ref, box_ref, twiddle_ref, src_ref, slot_vmem, slot_smem, sems,
+    owner_ref, box_ref, twiddle_ref, src_ref, slot_vmem, slot_smem, hits, parts, sems,
 ):
     pairs = (
         (owner_hbm, owner_ref), (box_hbm, box_ref), (twiddle_hbm, twiddle_ref), (src_hbm, src_ref),
@@ -107,7 +103,6 @@
     target_high = jnp.right_shift(target, 5)
     target_low = jnp.bitwise_and(target, 31)
     count = jnp.zeros((devices, 1), jnp.float32)
-    labels = jnp.zeros((devices, LANES), jnp.float32)
     for c in range(chunks):
         dest_c = dest[c : c + 1, :]
         hit = dest_c == rows
@@ -121,10 +116,12 @@
         slot_vmem[c : c + 1, :] = dest_c * SLOTS + jnp.where(now, rank, LABEL_ROW)
         part = jnp.where(high_half, target_high[c : c + 1, :], target_low[c : c + 1, :])
         part = jnp.where(rank == rank_of_row, part, 0).astype(jnp.float32).astype(jnp.bfloat16)
-        labels = labels + lax.dot_general(
-            onehot, part, (((1,), (1,)), ((), ())), preferred_element_type=jnp.float32
-        )
+        hits[:, c * LANES : (c + 1) * LANES] = onehot
+        parts[:, c * LANES : (c + 1) * LANES] = part
     copies[4].start()
+    labels = lax.dot_general(
+        hits[...], parts[...], (((1,), (1,)), ((), ())), preferred_element_type=jnp.float32
+    )
     copies[2].wait()
     angle_rows = sum(angles_for_all(twiddle_ref, n, lane) for n, lane in enumerate(ANGLE_LANES))
     passes = kept(rows)
@@ -187,6 +184,8 @@
             pltpu.VMEM(sources.shape, jnp.float32),
             block,
             pltpu.SMEM((chunks, LANES), jnp.int32),
+            pltpu.VMEM((LANES, count), jnp.bfloat16),
+            pltpu.VMEM((LANES, count), jnp.bfloat16),
             pltpu.SemaphoreType.DMA((5,)),
         ],
         compiler_params=params(),
@@ -241,12 +240,9 @@
 
 def picked(held, row, column):
     pick = jnp.where(row == iota((held.shape[0], 8 * LANES), 0), 1.0, 0.0).astype(jnp.bfloat16)
-    high = held.astype(jnp.bfloat16)
-    rest = held - high.astype(jnp.float32)
-    parts = (high, *split(rest))
     spread = sum(
         lax.dot_general(part, pick, (((0,), (0,)), ((), ())), preferred_element_type=jnp.float32)
-        for part in parts
+        for part in thirds(held)
     )
     mine = column == iota((LANES, 8 * LANES), 0)
     angle = jnp.sum(jnp.where(mine, spread, 0.0), axis=0, keepdims=True)

time: 63.7 us -> 63.5 us (level)
  no operation moved by 1% of the time
where the time goes in v5:
time: 63.5 us; the launch traced here: 63 us
  waiting for transfers between devices  26.5 us (42%)
  Pallas kernels  17.6 us (28%)
  starting transfers between devices  14.8 us (23%)
  local copies, waits for them, and re-layouts  3.01 us (5%)
  between operations  0.86 us (1%)
    ppermute x3, waiting for transfers between devices, swapped(): lax.ppermute(shard, axis, [(i, i ^ shift) for i in range(lax.axis_size(ax...  22.5 us
    all_to_all x1, starting transfers between devices, deliver(): lax.all_to_all(packed.reshape(-1, SLOTS, width), ('gx', 'gy'), split_axis...  11.5 us
    pallas_call x1, Pallas kernels, finish(): pl.pallas_call(finish_kernel, out_shape=[jax.ShapeDtypeStruct((box_count,...  8.74 us
    pallas_call x1, Pallas kernels, prepare(): pl.pallas_call(prepare_kernel, out_shape=[jax.ShapeDtypeStruct((levels *...  4.47 us
    pallas_call x1, Pallas kernels, pack(): pl.pallas_call(pack_kernel, out_shape=jax.ShapeDtypeStruct((LANES * SLOTS...  4.42 us
    all_to_all x1, waiting for transfers between devices, deliver(): lax.all_to_all(packed.reshape(-1, SLOTS, width), ('gx', 'gy'), split_axis...  3.93 us
    ppermute x3, starting transfers between devices, swapped(): lax.ppermute(shard, axis, [(i, i ^ shift) for i in range(lax.axis_size(ax...  3.35 us
    unnamed x12, local copies, waits for them, and re-layouts  3.01 us
  transfers between devices with their start and end apart: 4, of which 2 were waited for; matrix products, arithmetic and copies ran while one was open for 0% of the time, Pallas kernels for 7%

profile of v5, /device:TPU:1, one launch (start us, length us, event | category | flops | bytes accessed | tf_op | source)
XLA Modules:
  0.0 63.0 jit_solution(13958183504302832698)
XLA Ops:
  0.0 4.4 %shard_map.66 = f32[5120,128]{1,0:T(8,128)S(1)} custom-call(s32[1]{0:T(128)} %constant.36.clone.1.round_ref, s32[1]{0:T(128)} %bitcast.7.dev_ref, s32[16,128]{1,0:T(8,128)} %bitcast.30, s32[16,128]{1,0:T(8,128)} %bitcast.32, f32[7,1024]{1,0:T(8,128)} %peer0.1, f32[2048,128]{1,0:T(8,128)} %src_hbm.1), custom_call_target="tpu_custom_call" | custom-call | tf_op jit(solution)/shard_map/pallas_call | solution.py:175
  4.4 0.0 copy-start.2
  4.4 1.5 %copy-done.2 = f32[5120,128]{1,0:T(8,128)} copy-done((f32[5120,128]{1,0:T(8,128)}, f32[5120,128]{1,0:T(8,128)S(1)}, u32[]{:S(2)}) %copy-start.2) | copy-done | bytes 2621464
  5.9 0.0 copy-start.6
  5.9 0.0 copy-start.4
  5.9 11.5 %all-to-all-start.1 = ((f32[128,40,128]{2,1,0:T(8,128)}), f32[128,40,128]{2,1,0:T(8,128)S(1)}, u32[]{:S(2)}, u32[]{:S(2)}) async-start(f32[128,40,128]{2,1,0:T(8,128)} %bitcast.29), calls=%async_computation.1 | async-start | bytes 5242880 | tf_op jit(solution)/shard_map/all_to_all | solution.py:204
  17.4 0.0 copy-done.6
  17.5 2.7 %collective-permute-start.2 = (f32[7,1024]{1,0:T(8,128)S(1)}, f32[7,1024]{1,0:T(8,128)S(1)}, u32[]{:S(2)}, u32[]{:S(2)}) collective-permute-start(f32[7,1024]{1,0:T(8,128)S(1)} %copy-done.6), channel_id=1, source_target_pairs={{0,96},{8,104},{16,112},{24,120},{32,64},{40,72},{48,80},{56,88},{... | collective-permute-start | bytes 86024 | tf_op jit(solution)/shard_map/ppermute | solution.py:13
  20.1 0.6 collective-permute-start.1
  20.7 0.1 collective-permute-start
  20.8 0.0 copy-done.4
  20.8 0.0 copy-start.3
  20.8 1.5 %copy-done.3 = f32[7,2,2,2,64,64]{5,4,3,2,1,0:T(8,128)S(1)} copy-done((f32[7,2,2,2,64,64]{5,4,3,2,1,0:T(8,128)S(1)}, f32[7,2,2,2,64,64]{5,4,3,2,1,0:T(8,128)}, u32[]{:S(2)}) %copy-start.3) | copy-done | bytes 917528
  22.3 4.5 %shard_map.67 = (f32[56,128]{1,0:T(8,128)S(1)}, f32[56,128]{1,0:T(8,128)S(1)}, bf16[128,128]{1,0:T(8,128)(2,1)S(1)}, bf16[128,128]{1,0:T(8,128)(2,1)S(1)}, bf16[...) custom-call(s32[1]{0:T(128)} %bitcast.7.dev_ref, f32[7,1024]{1,0:T(8,128)S(1)} %copy-done.6, ...), custom_call_target="tpu_custom_call" | custom-call | tf_op jit(solution)/shard_map/pallas_call | solution.py:293
  26.8 0.0 copy-start.8
  26.8 0.0 copy-start.9
  26.8 22.5 %collective-permute-done.2.peer3 = f32[7,1024]{1,0:T(8,128)S(1)} collective-permute-done((f32[7,1024]{1,0:T(8,128)S(1)}, f32[7,1024]{1,0:T(8,128)S(1)}, u32[]{:S(2)}, u32[]{:S(2)}) %collective-permute-start.2) | collective-permute-done | bytes 28704 | tf_op jit(solution)/shard_map/ppermute | solution.py:13
  49.3 0.0 collective-permute-done.1.peer2
  49.3 0.0 collective-permute-done.peer1
  49.3 3.9 %all-to-all-done.1 = f32[128,40,128]{2,1,0:T(8,128)S(1)} async-done(((f32[128,40,128]{2,1,0:T(8,128)}), f32[128,40,128]{2,1,0:T(8,128)S(1)}, u32[]{:S(2)}, u32[]{:S(2)}) %all-to-all-start.1) | async-done | bytes 2621472 | tf_op jit(solution)/shard_map/all_to_all | solution.py:204
  53.2 8.7 %shard_map.68 = (f32[1024,128]{1,0:T(8,128)}, s32[1]{0:T(128)}, f32[56,128]{1,0:T(8,128)}, f32[56,128]{1,0:T(8,128)}) custom-call(s32[1]{0:T(128)} %bitcast.7.dev_ref, f32[5120,128]{1,0:T(8,128)S(1)} %bitcast.28, f32[7,1024]{1,0:T(8,128)S(1)} %copy-done.6, f32[7,1024]{1,0:T(8,128)S(1)} %collective-permute-done.peer1, ...), custom_call_target="tpu_custom_call" | custom-call | tf_op jit(solution)/shard_map/pallas_call | solution.py:463
  62.6 0.0 copy-done.8
  62.6 0.0 copy-done.9
  62.6 0.2 conditional.1
Async XLA Ops:
  4.4 1.5 %copy-start.2 = (f32[5120,128]{1,0:T(8,128)}, f32[5120,128]{1,0:T(8,128)S(1)}, u32[]{:S(2)}) copy-start(f32[5120,128]{1,0:T(8,128)S(1)} %shard_map.66) | copy-start | bytes 7864324
  5.9 11.5 %copy-start.6 = (f32[7,1024]{1,0:T(8,128)S(1)}, f32[7,1024]{1,0:T(8,128)}, u32[]{:S(2)}) copy-start(f32[7,1024]{1,0:T(8,128)} %peer0.1) | copy-start | bytes 86020
  5.9 14.9 %copy-start.4 = (f32[2,64,64]{2,1,0:T(8,128)S(1)}, f32[2,64,64]{2,1,0:T(8,128)}, u32[]{:S(2)}) copy-start(f32[2,64,64]{2,1,0:T(8,128)} %leaf_ref.1) | copy-start | bytes 98308
  5.9 47.3 %all-to-all-start.1 = ((f32[128,40,128]{2,1,0:T(8,128)}), f32[128,40,128]{2,1,0:T(8,128)S(1)}, u32[]{:S(2)}, u32[]{:S(2)}) async-start(f32[128,40,128]{2,1,0:T(8,128)} %bitcast.29), calls=%async_computation.1 | async-start | bytes 5242880 | tf_op jit(solution)/shard_map/all_to_all | solution.py:204
  17.5 31.8 %collective-permute-start.2 = (f32[7,1024]{1,0:T(8,128)S(1)}, f32[7,1024]{1,0:T(8,128)S(1)}, u32[]{:S(2)}, u32[]{:S(2)}) collective-permute-start(f32[7,1024]{1,0:T(8,128)S(1)} %copy-done.6), channel_id=1, source_target_pairs={{0,96},{8,104},{16,112},{24,120},{32,64},{40,72},{48,80},{56,88},{... | collective-permute-start | bytes 86024 | tf_op jit(solution)/shard_map/ppermute | solution.py:13
  20.1 29.2 %collective-permute-start.1 = (f32[7,1024]{1,0:T(8,128)S(1)}, f32[7,1024]{1,0:T(8,128)S(1)}, u32[]{:S(2)}, u32[]{:S(2)}) collective-permute-start(f32[7,1024]{1,0:T(8,128)S(1)} %copy-done.6), channel_id=1, source_target_pairs={{0,64},{8,72},{16,80},{24,88},{32,96},{40,104},{48,112},{56,120},{... | collective-permute-start | bytes 86024 | tf_op jit(solution)/shard_map/ppermute | solution.py:13
  20.7 28.6 %collective-permute-start = (f32[7,1024]{1,0:T(8,128)S(1)}, f32[7,1024]{1,0:T(8,128)S(1)}, u32[]{:S(2)}, u32[]{:S(2)}) collective-permute-start(f32[7,1024]{1,0:T(8,128)S(1)} %copy-done.6), channel_id=1, source_target_pairs={{0,32},{8,40},{16,48},{24,56},{32,0},{40,8},{48,16},{56,24},{64,96... | collective-permute-start | bytes 86024 | tf_op jit(solution)/shard_map/ppermute | solution.py:13
  20.8 1.5 %copy-start.3 = (f32[7,2,2,2,64,64]{5,4,3,2,1,0:T(8,128)S(1)}, f32[7,2,2,2,64,64]{5,4,3,2,1,0:T(8,128)}, u32[]{:S(2)}) copy-start(f32[7,2,2,2,64,64]{5,4,3,2,1,0:T(8,128)} %ops_ref.1) | copy-start | bytes 2752516
  26.8 35.9 %copy-start.8 = (s32[2048,1]{0,1:T(1,128)S(1)}, s32[2048,1]{0,1:T(1,128)}, u32[]{:S(2)}) copy-start(s32[2048,1]{0,1:T(1,128)} %param.11) | copy-start | bytes 24580
  26.8 35.9 %copy-start.9 = (s32[2048]{0:T(1024)S(1)}, s32[2048]{0:T(1024)}, u32[]{:S(2)}) copy-start(s32[2048]{0:T(1024)} %param.12) | copy-start | bytes 24580

commit v6 on v5

--- a/solution.py
+++ b/solution.py
@@ -256,7 +256,7 @@
 
 
 def prepare_kernel(
-    dev_ref, twiddle_ref, leaf_ref, ops_ref, cos_ref, sin_ref, leaf_h, leaf_l, mats_h, mats_l
+    dev_ref, twiddle_ref, leaf_ref, ops_ref, cos_ref, sin_ref, mats_h, mats_l
 ):
     cos_ref[0:48, :] = jnp.zeros((48, LANES), jnp.float32)
     sin_ref[0:48, :] = jnp.zeros((48, LANES), jnp.float32)
@@ -273,11 +273,14 @@
         return jnp.concatenate([top, bottom], axis=0).T
 
     leaf = block(leaf_ref[0], leaf_ref[1])
-    leaf_h[...], leaf_l[...] = split(leaf)
 
     def build(n, carry):
         level, e, c = n // 4, lax.rem(n, 4) // 2, lax.rem(n, 2)
-        high, low = split(block(ops_ref[level, e, c, 0], ops_ref[level, e, c, 1]))
+        matrix = block(ops_ref[level, e, c, 0], ops_ref[level, e, c, 1])
+        led = jnp.dot(
+            matrix, leaf, precision=lax.Precision.HIGHEST, preferred_element_type=jnp.float32
+        )
+        high, low = split(jnp.where(level == 0, led, matrix))
         out = pl.ds(pl.multiple_of(e * LANES, LANES), LANES)
         across = pl.ds(pl.multiple_of(c * LANES, LANES), LANES)
         mats_h[level, out, across] = high
@@ -295,13 +298,11 @@
         out_shape=[
             jax.ShapeDtypeStruct((levels * count // LANES, LANES), jnp.float32),
             jax.ShapeDtypeStruct((levels * count // LANES, LANES), jnp.float32),
-            jax.ShapeDtypeStruct((width, width), jnp.bfloat16),
-            jax.ShapeDtypeStruct((width, width), jnp.bfloat16),
             jax.ShapeDtypeStruct((levels, 2 * width, 2 * width), jnp.bfloat16),
             jax.ShapeDtypeStruct((levels, 2 * width, 2 * width), jnp.bfloat16),
         ],
         in_specs=in_smem() + in_vmem(3),
-        out_specs=in_vmem(6),
+        out_specs=in_vmem(4),
         compiler_params=params(),
     )(own_number(), twiddle, leaf_op, level_ops)
 
@@ -406,12 +407,12 @@
 
 def finish_kernel(
     dev_ref, x_ref, peer0, peer1, peer2, peer3,
-    cos_in, sin_in, leaf_h_in, leaf_l_in, mats_h_in, mats_l_in,
+    cos_in, sin_in, mats_h_in, mats_l_in,
     out_ref, flag_ref, cos_ref, sin_ref,
-    sums, names, cos_far, sin_far, leaf_h, leaf_l, mats_h, mats_l, sems,
+    sums, names, cos_far, sin_far, mats_h, mats_l, sems,
 ):
     pairs = (
-        (cos_in, cos_far), (sin_in, sin_far), (leaf_h_in, leaf_h), (leaf_l_in, leaf_l),
+        (cos_in, cos_far), (sin_in, sin_far),
         (mats_h_in, mats_h), (mats_l_in, mats_l),
     )
     copies = [pltpu.make_async_copy(a, b, sems.at[n]) for n, (a, b) in enumerate(pairs)]
@@ -442,8 +443,6 @@
     for c in range(8):
         block = sums[c * LANES : (c + 1) * LANES, :]
         state.append((block[:, :LANES] + block[:, LANES:]).T)
-    leafed = product(leaf_h[...], leaf_l[...], jnp.concatenate(state, axis=1))
-    state = [leafed[:, c * LANES : (c + 1) * LANES] for c in range(8)]
     done = 0
     for number in range(7):
         mask = nibble(MASKS, number)
@@ -468,7 +467,7 @@
             table,
             table,
         ],
-        in_specs=in_smem() + in_vmem(5) + anywhere(6),
+        in_specs=in_smem() + in_vmem(5) + anywhere(4),
         out_specs=in_vmem(1) + in_smem() + in_vmem(2),
         scratch_shapes=[
             pltpu.VMEM((box_count, 2 * width), jnp.float32),
@@ -508,15 +507,15 @@
     )(arrived, sums)
 
 
-def levels_kernel(sums, cos_ref, sin_ref, leaf_h, leaf_l, mats_h, mats_l, out_ref, state):
+def levels_kernel(sums, cos_ref, sin_ref, mats_h, mats_l, out_ref, state):
     half = LANES // 2
 
-    def leaf(c, carry):
+    def turn(c, carry):
         block = sums[pl.ds(pl.multiple_of(c * LANES, LANES), LANES), :]
-        state[c] = product(leaf_h[...], leaf_l[...], (block[:, :LANES] + block[:, LANES:]).T)
-        return carry
-
-    lax.fori_loop(0, 8, leaf, 0)
+        state[c] = (block[:, :LANES] + block[:, LANES:]).T
+        return carry
+
+    lax.fori_loop(0, 8, turn, 0)
 
     def level(number, carry):
         pairs = chunk_pairs(nibble(MASKS, number))
@@ -563,7 +562,7 @@
     return pl.pallas_call(
         levels_kernel,
         out_shape=jax.ShapeDtypeStruct((box_count, width), jnp.float32),
-        in_specs=in_vmem(7),
+        in_specs=in_vmem(5),
         out_specs=in_vmem(1)[0],
         scratch_shapes=[pltpu.VMEM((8, width, LANES), jnp.float32)],
         compiler_params=params(),

time: 63.5 us -> 63.3 us (level)
  Pallas kernels: 17.6 us -> 21.6 us
  waiting for transfers between devices: 26.5 us -> 22.6 us
    pallas_call x1, Pallas kernels: 4.47 us -> 8.35 us  [prepare(): pl.pallas_call(prepare_kernel, out_shape=[jax.ShapeDtypeStruct((levels *...]
    ppermute x3, waiting for transfers between devices: 22.5 us -> 18.6 us  [swapped(): lax.ppermute(shard, axis, [(i, i ^ shift) for i in range(lax.axis_size(ax...]
  transfers between devices with their start and end apart: 4 -> 4, of which waited for: 2 -> 2; matrix products, arithmetic and copies ran while one was open for 0% -> 0% of each run, Pallas kernels for 7% -> 13%
where the time goes in v6:
time: 63.3 us; the launch traced here: 63 us
  waiting for transfers between devices  22.6 us (36%)
  Pallas kernels  21.6 us (34%)
  starting transfers between devices  14.8 us (23%)
  local copies, waits for them, and re-layouts  3.01 us (5%)
  between operations  0.85 us (1%)
    ppermute x3, waiting for transfers between devices, swapped(): lax.ppermute(shard, axis, [(i, i ^ shift) for i in range(lax.axis_size(ax...  18.6 us
    all_to_all x1, starting transfers between devices, deliver(): lax.all_to_all(packed.reshape(-1, SLOTS, width), ('gx', 'gy'), split_axis...  11.5 us
    pallas_call x1, Pallas kernels, finish(): pl.pallas_call(finish_kernel, out_shape=[jax.ShapeDtypeStruct((box_count,...  8.78 us
    pallas_call x1, Pallas kernels, prepare(): pl.pallas_call(prepare_kernel, out_shape=[jax.ShapeDtypeStruct((levels *...  8.35 us
    pallas_call x1, Pallas kernels, pack(): pl.pallas_call(pack_kernel, out_shape=jax.ShapeDtypeStruct((LANES * SLOTS...  4.42 us
    all_to_all x1, waiting for transfers between devices, deliver(): lax.all_to_all(packed.reshape(-1, SLOTS, width), ('gx', 'gy'), split_axis...  3.93 us
    ppermute x3, starting transfers between devices, swapped(): lax.ppermute(shard, axis, [(i, i ^ shift) for i in range(lax.axis_size(ax...  3.35 us
    unnamed x12, local copies, waits for them, and re-layouts  3.01 us
  transfers between devices with their start and end apart: 4, of which 2 were waited for; matrix products, arithmetic and copies ran while one was open for 0% of the time, Pallas kernels for 13%

profile of v6, /device:TPU:1, one launch (start us, length us, event | category | flops | bytes accessed | tf_op | source)
XLA Modules:
  0.0 63.0 jit_solution(7526858264264148679)
XLA Ops:
  0.0 4.4 %shard_map.66 = f32[5120,128]{1,0:T(8,128)S(1)} custom-call(s32[1]{0:T(128)} %constant.36.clone.1.round_ref, s32[1]{0:T(128)} %bitcast.7.dev_ref, s32[16,128]{1,0:T(8,128)} %bitcast.30, s32[16,128]{1,0:T(8,128)} %bitcast.32, f32[7,1024]{1,0:T(8,128)} %peer0.1, f32[2048,128]{1,0:T(8,128)} %src_hbm.1), custom_call_target="tpu_custom_call" | custom-call | tf_op jit(solution)/shard_map/pallas_call | solution.py:175
  4.4 0.0 copy-start.2
  4.4 1.5 %copy-done.2 = f32[5120,128]{1,0:T(8,128)} copy-done((f32[5120,128]{1,0:T(8,128)}, f32[5120,128]{1,0:T(8,128)S(1)}, u32[]{:S(2)}) %copy-start.2) | copy-done | bytes 2621464
  5.9 0.0 copy-start.6
  5.9 0.0 copy-start.4
  5.9 11.5 %all-to-all-start.1 = ((f32[128,40,128]{2,1,0:T(8,128)}), f32[128,40,128]{2,1,0:T(8,128)S(1)}, u32[]{:S(2)}, u32[]{:S(2)}) async-start(f32[128,40,128]{2,1,0:T(8,128)} %bitcast.29), calls=%async_computation.1 | async-start | bytes 5242880 | tf_op jit(solution)/shard_map/all_to_all | solution.py:204
  17.4 0.0 copy-done.6
  17.4 2.7 %collective-permute-start.2 = (f32[7,1024]{1,0:T(8,128)S(1)}, f32[7,1024]{1,0:T(8,128)S(1)}, u32[]{:S(2)}, u32[]{:S(2)}) collective-permute-start(f32[7,1024]{1,0:T(8,128)S(1)} %copy-done.6), channel_id=1, source_target_pairs={{0,96},{8,104},{16,112},{24,120},{32,64},{40,72},{48,80},{56,88},{... | collective-permute-start | bytes 86024 | tf_op jit(solution)/shard_map/ppermute | solution.py:13
  20.1 0.6 collective-permute-start.1
  20.7 0.1 collective-permute-start
  20.8 0.0 copy-done.4
  20.8 0.0 copy-start.3
  20.8 1.5 %copy-done.3 = f32[7,2,2,2,64,64]{5,4,3,2,1,0:T(8,128)S(1)} copy-done((f32[7,2,2,2,64,64]{5,4,3,2,1,0:T(8,128)S(1)}, f32[7,2,2,2,64,64]{5,4,3,2,1,0:T(8,128)}, u32[]{:S(2)}) %copy-start.3) | copy-done | bytes 917528
  22.3 8.4 %shard_map.67 = (f32[56,128]{1,0:T(8,128)S(1)}, f32[56,128]{1,0:T(8,128)S(1)}, bf16[7,256,256]{2,1,0:T(8,128)(2,1)}, bf16[7,256,256]{2,1,0:T(8,128)(2,1)}) custom-call(s32[1]{0:T(128)} %bitcast.7.dev_ref, f32[7,1024]{1,0:T(8,128)S(1)} %copy-done.6, f32[2,64,64]{2,1,0:T(8,128)S(1)} %copy-done.4, f32[7,2,2,2,64,64]{5,4,3,2,1,0:T(8,128)S(1)} %copy-done.3), custom_call_target="tpu_custom_call" | custom-call | tf_op jit(solution)/shard_map/pallas_call | solution.py:296
  30.7 0.0 copy-start.8
  30.7 0.0 copy-start.9
  30.7 18.6 %collective-permute-done.2.peer3 = f32[7,1024]{1,0:T(8,128)S(1)} collective-permute-done((f32[7,1024]{1,0:T(8,128)S(1)}, f32[7,1024]{1,0:T(8,128)S(1)}, u32[]{:S(2)}, u32[]{:S(2)}) %collective-permute-start.2) | collective-permute-done | bytes 28704 | tf_op jit(solution)/shard_map/ppermute | solution.py:13
  49.3 0.0 collective-permute-done.1.peer2
  49.3 0.0 collective-permute-done.peer1
  49.3 3.9 %all-to-all-done.1 = f32[128,40,128]{2,1,0:T(8,128)S(1)} async-done(((f32[128,40,128]{2,1,0:T(8,128)}), f32[128,40,128]{2,1,0:T(8,128)S(1)}, u32[]{:S(2)}, u32[]{:S(2)}) %all-to-all-start.1) | async-done | bytes 2621472 | tf_op jit(solution)/shard_map/all_to_all | solution.py:204
  53.2 8.8 %shard_map.68 = (f32[1024,128]{1,0:T(8,128)}, s32[1]{0:T(128)}, f32[56,128]{1,0:T(8,128)}, f32[56,128]{1,0:T(8,128)}) custom-call(s32[1]{0:T(128)} %bitcast.7.dev_ref, f32[5120,128]{1,0:T(8,128)S(1)} %bitcast.28, f32[7,1024]{1,0:T(8,128)S(1)} %copy-done.6, f32[7,1024]{1,0:T(8,128)S(1)} %collective-permute-done.peer1, ...), custom_call_target="tpu_custom_call" | custom-call | tf_op jit(solution)/shard_map/pallas_call | solution.py:462
  62.6 0.0 copy-done.8
  62.7 0.0 copy-done.9
  62.7 0.2 conditional.1
Async XLA Ops:
  4.4 1.5 %copy-start.2 = (f32[5120,128]{1,0:T(8,128)}, f32[5120,128]{1,0:T(8,128)S(1)}, u32[]{:S(2)}) copy-start(f32[5120,128]{1,0:T(8,128)S(1)} %shard_map.66) | copy-start | bytes 7864324
  5.9 11.5 %copy-start.6 = (f32[7,1024]{1,0:T(8,128)S(1)}, f32[7,1024]{1,0:T(8,128)}, u32[]{:S(2)}) copy-start(f32[7,1024]{1,0:T(8,128)} %peer0.1) | copy-start | bytes 86020
  5.9 14.9 %copy-start.4 = (f32[2,64,64]{2,1,0:T(8,128)S(1)}, f32[2,64,64]{2,1,0:T(8,128)}, u32[]{:S(2)}) copy-start(f32[2,64,64]{2,1,0:T(8,128)} %leaf_ref.1) | copy-start | bytes 98308
  5.9 47.3 %all-to-all-start.1 = ((f32[128,40,128]{2,1,0:T(8,128)}), f32[128,40,128]{2,1,0:T(8,128)S(1)}, u32[]{:S(2)}, u32[]{:S(2)}) async-start(f32[128,40,128]{2,1,0:T(8,128)} %bitcast.29), calls=%async_computation.1 | async-start | bytes 5242880 | tf_op jit(solution)/shard_map/all_to_all | solution.py:204
  17.4 31.8 %collective-permute-start.2 = (f32[7,1024]{1,0:T(8,128)S(1)}, f32[7,1024]{1,0:T(8,128)S(1)}, u32[]{:S(2)}, u32[]{:S(2)}) collective-permute-start(f32[7,1024]{1,0:T(8,128)S(1)} %copy-done.6), channel_id=1, source_target_pairs={{0,96},{8,104},{16,112},{24,120},{32,64},{40,72},{48,80},{56,88},{... | collective-permute-start | bytes 86024 | tf_op jit(solution)/shard_map/ppermute | solution.py:13
  20.1 29.2 %collective-permute-start.1 = (f32[7,1024]{1,0:T(8,128)S(1)}, f32[7,1024]{1,0:T(8,128)S(1)}, u32[]{:S(2)}, u32[]{:S(2)}) collective-permute-start(f32[7,1024]{1,0:T(8,128)S(1)} %copy-done.6), channel_id=1, source_target_pairs={{0,64},{8,72},{16,80},{24,88},{32,96},{40,104},{48,112},{56,120},{... | collective-permute-start | bytes 86024 | tf_op jit(solution)/shard_map/ppermute | solution.py:13
  20.7 28.6 %collective-permute-start = (f32[7,1024]{1,0:T(8,128)S(1)}, f32[7,1024]{1,0:T(8,128)S(1)}, u32[]{:S(2)}, u32[]{:S(2)}) collective-permute-start(f32[7,1024]{1,0:T(8,128)S(1)} %copy-done.6), channel_id=1, source_target_pairs={{0,32},{8,40},{16,48},{24,56},{32,0},{40,8},{48,16},{56,24},{64,96... | collective-permute-start | bytes 86024 | tf_op jit(solution)/shard_map/ppermute | solution.py:13
  20.8 1.5 %copy-start.3 = (f32[7,2,2,2,64,64]{5,4,3,2,1,0:T(8,128)S(1)}, f32[7,2,2,2,64,64]{5,4,3,2,1,0:T(8,128)}, u32[]{:S(2)}) copy-start(f32[7,2,2,2,64,64]{5,4,3,2,1,0:T(8,128)} %ops_ref.1) | copy-start | bytes 2752516
  30.7 32.0 %copy-start.8 = (s32[2048,1]{0,1:T(1,128)S(1)}, s32[2048,1]{0,1:T(1,128)}, u32[]{:S(2)}) copy-start(s32[2048,1]{0,1:T(1,128)} %param.11) | copy-start | bytes 24580
  30.7 32.0 %copy-start.9 = (s32[2048]{0:T(1024)S(1)}, s32[2048]{0:T(1024)}, u32[]{:S(2)}) copy-start(s32[2048]{0:T(1024)} %param.12) | copy-start | bytes 24580
